TPU v7x, 512 devices: a whole 4x4x16 slice. The times are simulated.
512 devices in a mesh: dp: 4 (over z_hi), node: 32 (over y, z_lo, core), chip: 4 (over x).
Axes of the slice: x: 4, y: 4, z: 16 (z_hi: 4, z_lo: 4; z = z_hi * 4 + z_lo), core: 2. Of those that a mesh axis runs over, the one named last changes fastest.
Arguments:
- se_gate: bfloat16 [65536, 2048], P(('dp', 'node', 'chip')), parts along dimension 0, may hold values from -6 to 6
- se_key: bfloat16 [65536, 2048], P(('dp', 'node', 'chip')), parts along dimension 0, may hold values from -6 to 6
- se_value: bfloat16 [65536, 2048], P(('dp', 'node', 'chip')), parts along dimension 0, may hold values from -6 to 6
- li_gate: bfloat16 [65536, 2048], P(('dp', 'node', 'chip')), parts along dimension 0, may hold values from -6 to 6
- li_key: bfloat16 [65536, 2048], P(('dp', 'node', 'chip')), parts along dimension 0, may hold values from -6 to 6
- li_value: bfloat16 [65536, 2048], P(('dp', 'node', 'chip')), parts along dimension 0, may hold values from -6 to 6
- se_feature: float32 [3, 3, 2048], replicated, may hold values from -3 to 3
- se_filter: float32 [7, 2048], replicated, may hold values from -2 to 2
- li_feature: float32 [3, 3, 2048], replicated, may hold values from -3 to 3
- li_residue: float32 [16, 2048], replicated, may hold values from -1.25 to 1.25
- li_rate: float32 [16, 2048], replicated, may hold values from 3.0517578e-06 to 0.08, as said below
- li_skip: float32 [2048], replicated, may hold values from -4 to 4
Outputs:
- se_out: bfloat16 [65536, 2048], P(('dp', 'node', 'chip')), parts along dimension 0
- li_out: bfloat16 [65536, 2048], P(('dp', 'node', 'chip')), parts along dimension 0
There are 4 independent parts, one for each index of `dp`. A program takes and returns all parts, laid end to end along the dimension named above; an argument that names none is the same for every part. Nothing has to cross between parts.
Inputs may be any that keep to these rules, and one draw needn't show every extreme that they name: `li_rate`: positive decay rates.
All inputs are finite; a program needn't handle non-finite values.
Results may differ from a plain program's by a relative error of at most 0.0055.
Values may be sent and summed in bfloat16 or wider, within the bound.
No kernel may reach another device: no remote copies, remote signals or barrier semaphores. Data moves between devices by JAX's collectives and lax.ppermute only.
A program may use at most 64 MiB of HBM per device.

v0:
```python
import functools

import jax
import jax.numpy as jnp
from jax import lax
from jax.experimental import pallas as pl
from jax.experimental.pallas import tpu as pltpu
from jax.sharding import Mesh, PartitionSpec as P

F32 = jnp.float32
BF16 = jnp.bfloat16
LANES = 128
NEAR = ("core", "chip")
FAR = "far"
PART = ("far", "core", "chip")
ROWS = 128
STEP = 16
GROUPS = ROWS // STEP
MODES = 16
VMEM_LIMIT = 16 * 1024 * 1024
HBM = pl.BlockSpec(memory_space=pltpu.HBM)
AUTO = None


SHORT_FLOPS = 50_000_000_000

def fast(*dims, dtype=F32):
    return pltpu.VMEM(dims, dtype)


def shape(*dims, dtype=F32):
    return jax.ShapeDtypeStruct(dims, dtype)


def slow(*dims, dtype=F32):
    return pltpu.HBM(dims, dtype)


def room(*dims, dtype=F32):
    return pltpu.VMEM(dims, dtype)


def call(kernel, name, ins, outs, scratch, flops, moved):
    whole = lambda spec: pl.BlockSpec(memory_space=pltpu.VMEM) if spec is None else spec
    many = len(outs) > 1
    inner = pl.pallas_call(
        kernel,
        out_shape=tuple(o for o, _ in outs) if many else outs[0][0],
        in_specs=[whole(spec) for spec in ins],
        out_specs=tuple(whole(spec) for _, spec in outs) if many else whole(outs[0][1]),
        name=name,
        scratch_shapes=list(scratch),
        compiler_params=pltpu.CompilerParams(vmem_limit_bytes=VMEM_LIMIT),
        cost_estimate=pl.CostEstimate(flops=flops, bytes_accessed=moved, transcendentals=0),
    )

    def outer(*values):
        return inner(
            *[pltpu.with_memory_space_constraint(v, pltpu.HBM) if spec is HBM else v for v, spec in zip(values, ins)]
        )

    return outer


def lanes_at(index):
    return pl.ds(pl.multiple_of(index * LANES, LANES), LANES)


def started(source, target, semaphore):
    copy = pltpu.make_async_copy(source, target, semaphore)
    copy.start()
    return copy


def pieces(width, count):
    size = width // count
    return [pl.ds(i * size, size) for i in range(count)]


def rim_kernel(seg, sek, sev, lig, lik, liv, after, out, tails, held, sems):
    del after
    copies = [started(ref.at[ROWS - 16 : ROWS], tails.at[i], sems.at[i]) for i, ref in enumerate((seg, sek, sev, lig, lik, liv))]
    held[24:32] = jnp.zeros_like(held[24:32])
    for copy in copies:
        copy.wait()
    held[0:8] = tails[1].astype(F32)[8:16]
    held[8:16] = tails[2].astype(F32)[8:16]
    held[16:18] = tails[0].astype(F32)[14:16]
    held[18:20] = tails[4].astype(F32)[14:16]
    held[20:22] = tails[5].astype(F32)[14:16]
    held[22:24] = tails[3].astype(F32)[14:16]
    out[...] = held[...].astype(BF16)


CHUNK = 8


def states_kernel(key_hbm, value_hbm, feature_hbm, rate_hbm, kept_hbm, sent_hbm, key, value, feature, rate, kept, sent, wide, fresh, sems, outs):
    width = key.shape[1]
    chunks = width // (CHUNK * LANES)
    spans = pieces(width, chunks)
    small = [started(feature_hbm, feature, sems.at[0]), started(rate_hbm, rate, sems.at[1])]
    large = [
        (
            started(key_hbm.at[:, span], key.at[:, span], sems.at[2 + 2 * i]),
            started(value_hbm.at[:, span], value.at[:, span], sems.at[3 + 2 * i]),
        )
        for i, span in enumerate(spans)
    ]
    for copy in small:
        copy.wait()

    def featurized(ref, stream, lanes, slot):
        raw = ref[:, lanes].astype(F32)
        wide[slot, stream, 8 : 8 + ROWS] = raw
        return (
            feature[0, stream : stream + 1, lanes] * raw
            + feature[1, stream : stream + 1, lanes] * wide[slot, stream, 7 : 7 + ROWS]
            + feature[2, stream : stream + 1, lanes] * wide[slot, stream, 6 : 6 + ROWS]
        )

    wide[:, :, 0:8] = jnp.zeros((2, 3, 8, LANES), F32)
    leaving = []
    for index in range(chunks):
        for copy in large[index]:
            copy.wait()
        decays = []
        for part in range(CHUNK):
            block = index * CHUNK + part
            lanes = pl.ds(block * LANES, LANES)
            owner = block // 2
            half = slice((part % 2) * LANES, (part % 2 + 1) * LANES)
            slot = part % 2
            u = featurized(key, 1, lanes, slot) * featurized(value, 2, lanes, slot)
            fresh[part] = u.astype(BF16).astype(F32)
            fresh[part, 0:2] = jnp.zeros((2, LANES), F32)
            sent[owner, 16:18, half] = wide[slot, 1, 8:10]
            sent[owner, 18:20, half] = wide[slot, 2, 8:10]
            sent[owner, 20:22, half] = wide[slot, 1, ROWS + 6 : ROWS + 8]
            sent[owner, 22:24, half] = wide[slot, 2, ROWS + 6 : ROWS + 8]
            decays.append(jnp.exp(-rate[:, lanes]))

        def group(g, states):
            for part in range(CHUNK):
                kept[g, :, pl.ds((index * CHUNK + part) * LANES, LANES)] = states[part]
            states = list(states)
            for t in range(STEP):
                for part in range(CHUNK):
                    row = fresh[part, pl.ds(g * STEP + t, 1), :]
                    states[part] = decays[part] * states[part] + row
            return tuple(states)

        zero = jnp.zeros((MODES, LANES), F32)
        states = lax.fori_loop(0, GROUPS, group, (zero,) * CHUNK)
        for part in range(CHUNK):
            half = slice((part % 2) * LANES, (part % 2 + 1) * LANES)
            sent[(index * CHUNK + part) // 2, 0:MODES, half] = states[part]
        owners = pl.ds(index * CHUNK // 2, CHUNK // 2)
        leaving.append(started(sent.at[owners], sent_hbm.at[owners], outs.at[2 * index]))
        leaving.append(started(kept.at[:, :, spans[index]], kept_hbm.at[:, :, spans[index]], outs.at[2 * index + 1]))
    for copy in leaving:
        copy.wait()


def first_two(taps, own, before):
    def pair(base, tap):
        zero, one = own[base : base + 1], own[base + 1 : base + 2]
        two_ago, one_ago = before[base : base + 1], before[base + 1 : base + 2]
        return (
            tap[0] * zero + tap[1] * one_ago + tap[2] * two_ago,
            tap[0] * one + tap[1] * zero + tap[2] * one_ago,
        )

    k0, k1 = pair(0, taps[0])
    v0, v1 = pair(2, taps[1])
    return ((k0 * v0).astype(BF16).astype(F32), (k1 * v1).astype(BF16).astype(F32))


def owned(feature, rate, chips):
    width = 2 * LANES
    me = lax.axis_index("core") * chips + lax.axis_index("chip")
    lanes = pl.ds(pl.multiple_of(me * width, width), width)
    taps = [[feature[j, s : s + 1, lanes] for j in range(3)] for s in (1, 2)]
    return taps, rate[:, lanes]


def group_kernel(chips, came, feature, rate, sent_hbm, full_hbm, sent, full, sems):
    taps, pace = owned(feature, rate, chips)
    e_block = jnp.exp(-float(ROWS) * pace)
    e_first = jnp.exp(-float(ROWS - 1) * pace)
    e_second = jnp.exp(-float(ROWS - 2) * pace)
    peers = came.shape[0]
    total = came[0, 0:MODES]
    full[0] = total
    for i in range(1, peers):
        u0, u1 = first_two(taps, came[i, 16:20], came[i - 1, 20:24])
        mine = came[i, 0:MODES] + e_first * u0 + e_second * u1
        full[i] = mine
        total = e_block * total + mine
    rims = jnp.concatenate([came[0, 16:20], came[peers - 1, 20:24]], axis=0)
    sent[...] = jnp.concatenate([total, rims], axis=0).astype(BF16)
    copies = [started(sent, sent_hbm.at[i], sems.at[i]) for i in range(sent_hbm.shape[0])]
    copies.append(started(full, full_hbm, sems.at[sent_hbm.shape[0]]))
    for copy in copies:
        copy.wait()


def carry_kernel(chips, came, full_hbm, feature, rate, out_hbm, full, out, sems):
    arriving = started(full_hbm, full, sems.at[0])
    taps, pace = owned(feature, rate, chips)
    me = lax.axis_index(FAR)
    peers = full.shape[0]
    span = float(ROWS * peers)
    e_group = jnp.exp(-span * pace)
    g_first = jnp.exp(-(span - 1.0) * pace)
    g_second = jnp.exp(-(span - 2.0) * pace)
    e_block = jnp.exp(-float(ROWS) * pace)
    e_first = jnp.exp(-float(ROWS - 1) * pace)
    e_second = jnp.exp(-float(ROWS - 2) * pace)
    carry = jnp.zeros_like(pace)
    before = jnp.zeros((4, pace.shape[1]), F32)
    own0 = jnp.zeros((1, pace.shape[1]), F32)
    own1 = own0
    for i in range(came.shape[0]):
        block = came[i].astype(F32)
        u0, u1 = first_two(taps, block[16:20], before)
        before = block[20:24]
        total = block[0:MODES] + g_first * u0 + g_second * u1
        carry = jnp.where(i < me, e_group * carry + total, carry)
        own0 = jnp.where(i == me, u0, own0)
        own1 = jnp.where(i == me, u1, own1)
    arriving.wait()
    out[0] = carry
    carry = e_block * carry + (full[0] + e_first * own0 + e_second * own1)
    for i in range(1, peers):
        out[i] = carry
        carry = e_block * carry + full[i]
    started(out, out_hbm, sems.at[1]).wait()


def reach_kernel(rate, weight, out):
    place = (lax.broadcasted_iota(jnp.int32, (STEP, LANES), 0) + 1).astype(F32)

    def block(index, carry):
        lanes = lanes_at(index)
        total = jnp.zeros((STEP, LANES), F32)
        for m in range(MODES):
            tap = weight[m : m + 1, lanes] * jnp.exp(-place * rate[m : m + 1, lanes])
            out[m, :, lanes] = tap
            total = total + tap
        out[MODES, :, lanes] = total
        now = jnp.sum(weight[:, lanes], axis=0, keepdims=True)
        out[MODES, STEP - 1 : STEP, lanes] = now
        return carry

    lax.fori_loop(0, rate.shape[1] // LANES, block, 0)


SHORT_PIECES = 4


def short_kernel(
    gate_hbm, key_hbm, value_hbm, rim_hbm, feature_hbm, taps_hbm, out_hbm, gate, key, value, rim, feature, taps, out, kw, vw, gw, uw, sems, outs
):
    width = key.shape[1]
    spans = pieces(width, SHORT_PIECES)
    small = [
        started(rim_hbm, rim, sems.at[0]),
        started(feature_hbm, feature, sems.at[1]),
        started(taps_hbm, taps, sems.at[2]),
    ]
    large = [
        [started(a.at[:, span], b.at[:, span], sems.at[3 + 3 * i + j]) for j, (a, b) in enumerate(((gate_hbm, gate), (key_hbm, key), (value_hbm, value)))]
        for i, span in enumerate(spans)
    ]
    for slot in range(2):
        kw[slot, 0:8] = jnp.zeros((8, LANES), F32)
        vw[slot, 0:8] = jnp.zeros((8, LANES), F32)
        gw[slot, 0:16] = jnp.zeros((16, LANES), F32)
    for copy in small:
        copy.wait()

    def one(block, slot):
        lanes = lanes_at(block)
        halo = rim[:, lanes].astype(F32)
        kw[slot, 8:16] = halo[0:8]
        kw[slot, 16 : 16 + ROWS] = key[:, lanes].astype(F32)
        vw[slot, 8:16] = halo[8:16]
        vw[slot, 16 : 16 + ROWS] = value[:, lanes].astype(F32)
        gw[slot, 14:16] = halo[16:18]
        gw[slot, 16 : 16 + ROWS] = gate[:, lanes].astype(F32)

        def feat(w, stream, start, count):
            f = [feature[j, stream : stream + 1, lanes] for j in range(3)]
            return (
                f[0] * w[slot, start : start + count]
                + f[1] * w[slot, start - 1 : start - 1 + count]
                + f[2] * w[slot, start - 2 : start - 2 + count]
            )

        u = feat(kw, 1, 8, ROWS + 8) * feat(vw, 2, 8, ROWS + 8)
        uw[slot] = u.astype(BF16).astype(F32)
        mixed = taps[0:1, lanes] * uw[slot, 8 : 8 + ROWS]
        for lag in range(1, taps.shape[0]):
            mixed = mixed + taps[lag : lag + 1, lanes] * uw[slot, 8 - lag : 8 - lag + ROWS]
        out[:, lanes] = (feat(gw, 0, 16, ROWS) * mixed).astype(BF16)

    each = width // SHORT_PIECES // LANES // 2
    leaving = []
    for i, span in enumerate(spans):
        for copy in large[i]:
            copy.wait()

        def pair(index, carry):
            for slot in range(2):
                one((i * each + index) * 2 + slot, slot)
            return carry

        lax.fori_loop(0, each, pair, 0)
        leaving.append(started(out.at[:, span], out_hbm.at[:, span], outs.at[i]))
    for copy in leaving:
        copy.wait()


LOCAL_PIECES = 4


def local_kernel(
    gate_hbm, key_hbm, value_hbm, rim_hbm, feature_hbm, skip_hbm, kept_hbm, reach, rate, out_hbm, out, gate, key, value, rim, feature, skip, kept, kw, vw, gw, uw, sems, outs
):
    width = key.shape[1]
    spans = pieces(width, LOCAL_PIECES)
    small = [
        started(rim_hbm, rim, sems.at[0]),
        started(feature_hbm, feature, sems.at[1]),
        started(skip_hbm, skip, sems.at[2]),
    ]
    large = [
        [
            started(a.at[:, span], b.at[:, span], sems.at[3 + 4 * i + j])
            for j, (a, b) in enumerate(((gate_hbm, gate), (key_hbm, key), (value_hbm, value)))
        ]
        + [started(kept_hbm.at[:, :, span], kept.at[:, :, span], sems.at[6 + 4 * i])]
        for i, span in enumerate(spans)
    ]
    for w in (kw, vw, gw, uw):
        for slot in range(2):
            w[slot, 0:16] = jnp.zeros((16, LANES), F32)
    place = lax.broadcasted_iota(jnp.int32, (STEP, LANES), 0)
    for copy in small:
        copy.wait()

    def one(block, slot):
        lanes = lanes_at(block)
        halo = rim[:, lanes].astype(F32)
        kw[slot, 14:16] = halo[18:20]
        kw[slot, 16 : 16 + ROWS] = key[:, lanes].astype(F32)
        vw[slot, 14:16] = halo[20:22]
        vw[slot, 16 : 16 + ROWS] = value[:, lanes].astype(F32)
        gw[slot, 14:16] = halo[22:24]
        gw[slot, 16 : 16 + ROWS] = gate[:, lanes].astype(F32)

        def feat(w, stream):
            f = [feature[j, stream : stream + 1, lanes] for j in range(3)]
            return f[0] * w[slot, 16 : 16 + ROWS] + f[1] * w[slot, 15 : 15 + ROWS] + f[2] * w[slot, 14 : 14 + ROWS]

        out[ROWS : 2 * ROWS, lanes] = feat(gw, 0)
        uw[slot, 16 : 16 + ROWS] = (feat(kw, 1) * feat(vw, 2)).astype(BF16).astype(F32)
        pace = rate[:, lanes]
        jump = jnp.exp(-float(STEP) * pace)
        state = uw[slot, 16:17] * jnp.exp(-float(STEP - 1) * pace) + uw[slot, 17:18] * jnp.exp(-float(STEP - 2) * pace)
        for g in range(1, GROUPS):
            out[2 * ROWS + g * MODES : 2 * ROWS + (g + 1) * MODES, lanes] = kept[g, :, lanes] + state
            state = state * jump
        now = reach[MODES, STEP - 1 : STEP, lanes] + skip[:, lanes]
        low, high = [], []
        for g in range(GROUPS):
            start = 16 + g * STEP
            low.append(now * uw[slot, start : start + 8])
            high.append(now * uw[slot, start + 8 : start + STEP])
        for lag in range(1, STEP):
            tap = jnp.where(place >= lag, reach[MODES, lag - 1 : lag, lanes], 0.0)
            for g in range(GROUPS):
                start = 16 + g * STEP - lag
                if lag < 8:
                    low[g] = low[g] + tap[0:8] * uw[slot, start : start + 8]
                high[g] = high[g] + tap[8:STEP] * uw[slot, start + 8 : start + STEP]
        for g in range(GROUPS):
            out[g * STEP : g * STEP + 8, lanes] = low[g]
            out[g * STEP + 8 : (g + 1) * STEP, lanes] = high[g]

    each = width // LOCAL_PIECES // LANES // 2
    leaving = []
    for i, span in enumerate(spans):
        for copy in large[i]:
            copy.wait()

        def pair(index, carry):
            for slot in range(2):
                one((i * each + index) * 2 + slot, slot)
            return carry

        lax.fori_loop(0, each, pair, 0)
        leaving.append(started(out.at[:, span], out_hbm.at[:, span], outs.at[i]))
    for copy in leaving:
        copy.wait()


FINISH_PIECES = 4


def finish_kernel(came, local_hbm, reach, rate, out_hbm, local, out, rows, sems, outs):
    width = rate.shape[1]
    spans = pieces(width, FINISH_PIECES)
    arriving = [started(local_hbm.at[:, span], local.at[:, span], sems.at[i]) for i, span in enumerate(spans)]
    each = width // FINISH_PIECES // LANES // 2

    def one(owner, slot):
        lanes = lanes_at(owner * 2 + slot)
        state = came[owner, :, slot * LANES : (slot + 1) * LANES]
        rows[slot, 0:MODES] = state
        jump = jnp.exp(-float(STEP) * rate[:, lanes])
        for g in range(1, GROUPS):
            state = state * jump
            rows[slot, g * MODES : (g + 1) * MODES] = state + local[2 * ROWS + g * MODES : 2 * ROWS + (g + 1) * MODES, lanes]
        totals = [local[g * STEP : (g + 1) * STEP, lanes] for g in range(GROUPS)]
        for m in range(MODES):
            tap = reach[m, :, lanes]
            for g in range(GROUPS):
                totals[g] = totals[g] + tap * rows[slot, g * MODES + m : g * MODES + m + 1]
        for g in range(GROUPS):
            total = local[ROWS + g * STEP : ROWS + (g + 1) * STEP, lanes] * totals[g]
            out[g * STEP : (g + 1) * STEP, lanes] = total.astype(BF16)

    leaving = []
    for i, span in enumerate(spans):

        def pair(index, carry):
            for slot in range(2):
                one(i * each + index, slot)
            return carry

        arriving[i].wait()
        lax.fori_loop(0, each, pair, 0)
        leaving.append(started(out.at[:, span], out_hbm.at[:, span], outs.at[i]))
    for copy in leaving:
        copy.wait()


def shards(
    se_gate,
    se_key,
    se_value,
    li_gate,
    li_key,
    li_value,
    se_feature,
    se_filter,
    li_feature,
    li_residue,
    li_rate,
    li_skip,
):
    width = se_gate.shape[1]
    chips = lax.axis_size("chip")
    near = lax.axis_size(NEAR)
    far = lax.axis_size(FAR)
    part = width // near
    swap = lambda value, axis: lax.all_to_all(value, axis, split_axis=0, concat_axis=0, tiled=True)
    dma = pltpu.SemaphoreType.DMA
    stream = room(ROWS, width, dtype=BF16)
    padded = room(2, 16 + ROWS, LANES)
    rim_room = room(32, width, dtype=BF16)
    feature_room = room(*li_feature.shape)

    kept, sent = call(
        states_kernel,
        "states",
        [HBM] * 4,
        [(slow(GROUPS, MODES, width), HBM), (slow(near, 24, part), HBM)],
        [
            stream,
            stream,
            feature_room,
            room(MODES, width),
            room(GROUPS, MODES, width),
            room(near, 24, part),
            room(2, 3, 8 + ROWS, LANES),
            room(CHUNK, ROWS, LANES),
            dma((2 + 2 * (width // (CHUNK * LANES)),)),
            dma((2 * (width // (CHUNK * LANES)),)),
        ],
        12000000,
        3000000,
    )(li_key, li_value, li_feature, li_rate)

    came = swap(sent, NEAR)
    rim = call(
        rim_kernel,
        "rim",
        [HBM] * 7,
        [(fast(32, width, dtype=BF16), AUTO)],
        [room(6, 16, width, dtype=BF16), room(32, width), dma((6,))],
        1000000,
        500000,
    )(se_gate, se_key, se_value, li_gate, li_key, li_value, kept)
    weight = li_residue * jnp.sqrt(-jnp.expm1(-2.0 * li_rate))
    reach = call(
        reach_kernel, "reach", [AUTO] * 2, [(fast(MODES + 1, STEP, width), AUTO)], [], 3000000, 2000000
    )(li_rate, weight)
    came, reach = lax.optimization_barrier((came, reach))

    group, full = call(
        functools.partial(group_kernel, chips),
        "group",
        [AUTO] * 3,
        [(slow(far, 24, part, dtype=BF16), HBM), (slow(near, MODES, part), HBM)],
        [room(24, part, dtype=BF16), room(near, MODES, part), dma((far + 1,))],
        500000,
        500000,
    )(came, li_feature, li_rate)

    groups = swap(group, FAR)
    count = lax.axis_size(PART)
    halo = lax.ppermute(rim, PART, [(i, i + 1) for i in range(count - 1)])
    se_out = call(
        short_kernel,
        "short",
        [HBM] * 6,
        [(slow(ROWS, width, dtype=BF16), HBM)],
        [
            stream,
            stream,
            stream,
            rim_room,
            feature_room,
            room(*se_filter.shape),
            stream,
            padded,
            padded,
            padded,
            room(2, 8 + ROWS, LANES),
            dma((3 + 3 * SHORT_PIECES,)),
            dma((SHORT_PIECES,)),
        ],
        SHORT_FLOPS,
        2000000,
    )(se_gate, se_key, se_value, halo, se_feature, se_filter)
    groups, se_out = lax.optimization_barrier((groups, se_out))

    states = call(
        functools.partial(carry_kernel, chips),
        "carry",
        [AUTO, HBM, AUTO, AUTO],
        [(slow(near, MODES, part), HBM)],
        [room(near, MODES, part), room(near, MODES, part), dma((2,))],
        500000,
        500000,
    )(groups, full, li_feature, li_rate)

    back = swap(states, NEAR)
    local = call(
        local_kernel,
        "local",
        [HBM] * 7 + [AUTO] * 2,
        [(slow(3 * ROWS, width), HBM)],
        [
            room(3 * ROWS, width),
            stream,
            stream,
            stream,
            rim_room,
            feature_room,
            room(1, width),
            room(GROUPS, MODES, width),
            padded,
            padded,
            padded,
            padded,
            dma((3 + 4 * LOCAL_PIECES,)),
            dma((LOCAL_PIECES,)),
        ],
        12000000,
        3000000,
    )(li_gate, li_key, li_value, halo, li_feature, li_skip.reshape(1, width), kept, reach, li_rate)

    li_out = call(
        finish_kernel,
        "finish",
        [AUTO, HBM, AUTO, AUTO],
        [(slow(ROWS, width, dtype=BF16), HBM)],
        [room(3 * ROWS, width), stream, room(2, GROUPS * MODES, LANES), dma((FINISH_PIECES,)), dma((FINISH_PIECES,))],
        10000000,
        5000000,
    )(back, local, reach, li_rate)
    return (se_out, li_out)


def solution(mesh):
    sizes = dict(zip(mesh.axis_names, mesh.devices.shape))
    split = mesh.devices.reshape(sizes["dp"], sizes["node"] // 2, 2, sizes["chip"])
    inner = Mesh(split, ("dp", "far", "core", "chip"))
    rows = P(("dp", "far", "core", "chip"), None)
    return jax.shard_map(
        shards,
        mesh=inner,
        in_specs=(rows,) * 6 + (P(),) * 6,
        out_specs=(rows, rows),
        check_vma=False,
    )
```

profile of v0, /device:TPU:1, one launch (start us, length us, event | category | flops | bytes accessed | tf_op | source)
XLA Modules:
  0.0 49.9 jit_solution(5925646782828930886)
XLA Ops:
  0.6 0.0 copy-start
  0.6 0.0 copy-start.3
  0.6 4.2 %states.1 = (f32[8,16,2048]{2,1,0:T(8,128)}, f32[8,24,256]{2,1,0:T(8,128)}) custom-call(bf16[128,2048]{1,0:T(8,128)(2,1)} %key_hbm.5, bf16[128,2048]{1,0:T(8,128)(2,1)} %value_hbm.5, f32[3,3,2048]{2,1,0:T(4,128)} %feature_hbm.5, f32[16,2048]{1,0:T(8,128)} %rate.9), custom_call_target="tpu_custom_call" | custom-call | flops 12000000 | bytes 3000000 | tf_op jit(solution)/shard_map/states/pallas_call | solution.py:58
  4.9 10.2 %all-to-all-start = ((f32[8,24,256]{2,1,0:T(8,128)}), f32[8,24,256]{2,1,0:T(8,128)S(1)}, u32[]{:S(2)}, u32[]{:S(2)}) async-start(f32[8,24,256]{2,1,0:T(8,128)} %get-tuple-element.10), calls=%async_computation | async-start | bytes 393216 | tf_op jit(solution)/shard_map/all_to_all | solution.py:469
  15.1 1.1 %rim.1 = bf16[32,2048]{1,0:T(8,128)(2,1)S(1)} custom-call(bf16[128,2048]{1,0:T(8,128)(2,1)} %gate_hbm.2, bf16[128,2048]{1,0:T(8,128)(2,1)} %key_hbm.4, bf16[128,2048]{1,0:T(8,128)(2,1)} %value_hbm.4, bf16[128,2048]{1,0:T(8,128)(2,1)} %gate_hbm.3, bf16[128,2048]{1,0:T(8,128)(2,1)} %key_hbm.5, bf16[128,2048]{1,0:T(8,128)(2,1)} %value_hbm.5, ...), custom_call_target="tpu_custom_call" | custom-call | flops 1000000 | bytes 500000 | tf_op jit(solution)/shard_map/rim/pallas_call | solution.py:58
  16.2 3.3 %collective-permute-start = (bf16[32,2048]{1,0:T(8,128)(2,1)S(1)}, bf16[32,2048]{1,0:T(8,128)(2,1)S(1)}, u32[]{:S(2)}, u32[]{:S(2)}) collective-permute-start(bf16[32,2048]{1,0:T(8,128)(2,1)S(1)} %rim.1), channel_id=1, source_target_pairs={{0,1},{1,2},{2,3},{3,4},{4,5},{5,6},{6,7},{7,8},{8,9},{9,10},{10,1... | collective-permute-start | bytes 393224 | tf_op jit(solution)/shard_map/ppermute | solution.py:525
  19.5 0.0 copy-done
  19.5 0.0 copy-done.3
  19.5 0.1 sqrt_multiply_fusion.weight
  19.6 0.6 %reach.1 = f32[17,16,2048]{2,1,0:T(8,128)S(1)} custom-call(f32[16,2048]{1,0:T(8,128)S(1)} %copy-done, f32[16,2048]{1,0:T(8,128)S(1)} %sqrt_multiply_fusion.weight), custom_call_target="tpu_custom_call" | custom-call | flops 3000000 | bytes 2000000 | tf_op jit(solution)/shard_map/reach/pallas_call | solution.py:58
  20.2 0.8 %all-to-all-done.came = f32[8,24,256]{2,1,0:T(8,128)S(1)} async-done(((f32[8,24,256]{2,1,0:T(8,128)}), f32[8,24,256]{2,1,0:T(8,128)S(1)}, u32[]{:S(2)}, u32[]{:S(2)}) %all-to-all-start) | async-done | bytes 196640 | tf_op jit(solution)/shard_map/all_to_all | solution.py:469
  21.0 0.0 copy-done.1
  21.0 0.9 %group.1 = (bf16[16,24,256]{2,1,0:T(8,128)(2,1)}, f32[8,16,256]{2,1,0:T(8,128)}) custom-call(f32[8,24,256]{2,1,0:T(8,128)S(1)} %all-to-all-done.came, f32[3,3,2048]{2,1,0:T(4,128)S(1)} %copy-done.1, f32[16,2048]{1,0:T(8,128)S(1)} %copy-done), custom_call_target="tpu_custom_call" | custom-call | flops 500000 | bytes 500000 | tf_op jit(solution)/shard_map/group/pallas_call | solution.py:58
  21.9 4.0 %all-to-all-start.1 = ((bf16[16,24,256]{2,1,0:T(8,128)(2,1)}), bf16[16,24,256]{2,1,0:T(8,128)(2,1)S(1)}, u32[]{:S(2)}, u32[]{:S(2)}) async-start(bf16[16,24,256]{2,1,0:T(8,128)(2,1)} %get-tuple-element.12), calls=%async_computation.1 | async-start | bytes 393216 | tf_op jit(solution)/shard_map/all_to_all | solution.py:469
  25.9 0.0 collective-permute-done.rim_hbm
  25.9 0.0 copy-start.2
  25.9 0.6 %copy-done.2 = bf16[32,2048]{1,0:T(8,128)(2,1)} copy-done((bf16[32,2048]{1,0:T(8,128)(2,1)}, bf16[32,2048]{1,0:T(8,128)(2,1)S(1)}, u32[]{:S(2)}) %copy-start.2) | copy-done | bytes 131096
  26.6 3.8 %short.1 = bf16[128,2048]{1,0:T(8,128)(2,1)} custom-call(bf16[128,2048]{1,0:T(8,128)(2,1)} %gate_hbm.2, bf16[128,2048]{1,0:T(8,128)(2,1)} %key_hbm.4, bf16[128,2048]{1,0:T(8,128)(2,1)} %value_hbm.4, bf16[32,2048]{1,0:T(8,128)(2,1)} %copy-done.2, f32[3,3,2048]{2,1,0:T(4,128)} %feature_hbm.4, f32[7,2048]{1,0:T(8,128)} %taps_hbm.1), custom_call_target="tpu_custom_call" | custom-call | flops 49999998976 | bytes 2000000 | tf_op jit(solution)/shard_map/short/pallas_call | solution.py:58
  30.3 3.1 %all-to-all-done.1.came = bf16[16,24,256]{2,1,0:T(8,128)(2,1)S(1)} async-done(((bf16[16,24,256]{2,1,0:T(8,128)(2,1)}), bf16[16,24,256]{2,1,0:T(8,128)(2,1)S(1)}, u32[]{:S(2)}, u32[]{:S(2)}) %all-to-all-start.1) | async-done | bytes 196640 | tf_op jit(solution)/shard_map/all_to_all | solution.py:469
  33.4 1.6 %carry.1 = f32[8,16,256]{2,1,0:T(8,128)} custom-call(bf16[16,24,256]{2,1,0:T(8,128)(2,1)S(1)} %all-to-all-done.1.came, f32[8,16,256]{2,1,0:T(8,128)} %get-tuple-element.16.full_hbm, f32[3,3,2048]{2,1,0:T(4,128)S(1)} %copy-done.1, f32[16,2048]{1,0:T(8,128)S(1)} %copy-done), custom_call_target="tpu_custom_call" | custom-call | flops 500000 | bytes 500000 | tf_op jit(solution)/shard_map/carry/pallas_call | solution.py:58
  35.0 6.2 %all-to-all-start.2 = ((f32[8,16,256]{2,1,0:T(8,128)}), f32[8,16,256]{2,1,0:T(8,128)S(1)}, u32[]{:S(2)}, u32[]{:S(2)}) async-start(f32[8,16,256]{2,1,0:T(8,128)} %carry.1), calls=%async_computation.2 | async-start | bytes 262144 | tf_op jit(solution)/shard_map/all_to_all | solution.py:469
  41.2 4.7 %local.1.local_hbm = f32[384,2048]{1,0:T(8,128)} custom-call(bf16[128,2048]{1,0:T(8,128)(2,1)} %gate_hbm.3, bf16[128,2048]{1,0:T(8,128)(2,1)} %key_hbm.5, bf16[128,2048]{1,0:T(8,128)(2,1)} %value_hbm.5, bf16[32,2048]{1,0:T(8,128)(2,1)} %copy-done.2, f32[3,3,2048]{2,1,0:T(4,128)} %feature_hbm.5, f32[1,2048]{1,0:T(1,128)} %bitcast.1, ...), custom_call_target="tpu_custom_call" | custom-call | flops 12000000 | bytes 3000000 | tf_op jit(solution)/shard_map/local/pallas_call | solution.py:58
  45.9 0.5 all-to-all-done.2.came
  46.4 3.5 %finish.1 = bf16[128,2048]{1,0:T(8,128)(2,1)} custom-call(f32[8,16,256]{2,1,0:T(8,128)S(1)} %all-to-all-done.2.came, f32[384,2048]{1,0:T(8,128)} %local.1.local_hbm, f32[17,16,2048]{2,1,0:T(8,128)S(1)} %reach.1, f32[16,2048]{1,0:T(8,128)S(1)} %copy-done), custom_call_target="tpu_custom_call" | custom-call | flops 10000000 | bytes 5000000 | tf_op jit(solution)/shard_map/finish/pallas_call | solution.py:58
  (1 shorter events, 0.0 us)
Async XLA Ops:
  0.6 18.9 %copy-start = (f32[16,2048]{1,0:T(8,128)S(1)}, f32[16,2048]{1,0:T(8,128)}, u32[]{:S(2)}) copy-start(f32[16,2048]{1,0:T(8,128)} %rate.9) | copy-start | bytes 393220
  0.6 18.9 %copy-start.3 = (f32[16,2048]{1,0:T(8,128)S(1)}, f32[16,2048]{1,0:T(8,128)}, u32[]{:S(2)}) copy-start(f32[16,2048]{1,0:T(8,128)} %param.21) | copy-start | bytes 393220
  4.9 16.1 %all-to-all-start = ((f32[8,24,256]{2,1,0:T(8,128)}), f32[8,24,256]{2,1,0:T(8,128)S(1)}, u32[]{:S(2)}, u32[]{:S(2)}) async-start(f32[8,24,256]{2,1,0:T(8,128)} %get-tuple-element.10), calls=%async_computation | async-start | bytes 393216 | tf_op jit(solution)/shard_map/all_to_all | solution.py:469
  15.1 5.9 %copy-start.1 = (f32[3,3,2048]{2,1,0:T(4,128)S(1)}, f32[3,3,2048]{2,1,0:T(4,128)}, u32[]{:S(2)}) copy-start(f32[3,3,2048]{2,1,0:T(4,128)} %feature_hbm.5) | copy-start | bytes 221188
  16.2 9.7 %collective-permute-start = (bf16[32,2048]{1,0:T(8,128)(2,1)S(1)}, bf16[32,2048]{1,0:T(8,128)(2,1)S(1)}, u32[]{:S(2)}, u32[]{:S(2)}) collective-permute-start(bf16[32,2048]{1,0:T(8,128)(2,1)S(1)} %rim.1), channel_id=1, source_target_pairs={{0,1},{1,2},{2,3},{3,4},{4,5},{5,6},{6,7},{7,8},{8,9},{9,10},{10,1... | collective-permute-start | bytes 393224 | tf_op jit(solution)/shard_map/ppermute | solution.py:525
  21.9 11.5 %all-to-all-start.1 = ((bf16[16,24,256]{2,1,0:T(8,128)(2,1)}), bf16[16,24,256]{2,1,0:T(8,128)(2,1)S(1)}, u32[]{:S(2)}, u32[]{:S(2)}) async-start(bf16[16,24,256]{2,1,0:T(8,128)(2,1)} %get-tuple-element.12), calls=%async_computation.1 | async-start | bytes 393216 | tf_op jit(solution)/shard_map/all_to_all | solution.py:469
  25.9 0.7 %copy-start.2 = (bf16[32,2048]{1,0:T(8,128)(2,1)}, bf16[32,2048]{1,0:T(8,128)(2,1)S(1)}, u32[]{:S(2)}) copy-start(bf16[32,2048]{1,0:T(8,128)(2,1)S(1)} %collective-permute-done.rim_hbm) | copy-start | bytes 393220
  35.0 11.4 %all-to-all-start.2 = ((f32[8,16,256]{2,1,0:T(8,128)}), f32[8,16,256]{2,1,0:T(8,128)S(1)}, u32[]{:S(2)}, u32[]{:S(2)}) async-start(f32[8,16,256]{2,1,0:T(8,128)} %carry.1), calls=%async_computation.2 | async-start | bytes 262144 | tf_op jit(solution)/shard_map/all_to_all | solution.py:469
where the time goes:
time: 50.4 us; the launch traced here: 49.9 us
  starting transfers between devices  23.7 us (47%)
  Pallas kernels  20.4 us (40%)
  waiting for transfers between devices  4.3 us (9%)
  between operations  0.76 us (2%)
  local copies, waits for them, and re-layouts  0.66 us (1%)
    pallas_call x8, Pallas kernels, outer(): inner(*[pltpu.with_memory_space_constraint(v, pltpu.HBM) if spec is HBM e...  20.4 us
    all_to_all x3, starting transfers between devices, shards(): lax.all_to_all(value, axis, split_axis=0, concat_axis=0, tiled=True)  20.4 us
    all_to_all x3, waiting for transfers between devices, shards(): lax.all_to_all(value, axis, split_axis=0, concat_axis=0, tiled=True)  4.3 us
    ppermute x1, starting transfers between devices, shards(): halo = lax.ppermute(rim, PART, [(i, i + 1) for i in range(count - 1)])  3.28 us
  transfers between devices with their start and end apart: 4, of which 3 were waited for; matrix products, arithmetic and copies ran while one was open for 0% of the time, Pallas kernels for 22%

commit v1 on v0

--- a/solution.py
+++ b/solution.py
@@ -16,13 +16,14 @@
 ROWS = 128
 STEP = 16
 GROUPS = ROWS // STEP
+HALF = STEP // 2
 MODES = 16
 VMEM_LIMIT = 16 * 1024 * 1024
 HBM = pl.BlockSpec(memory_space=pltpu.HBM)
 AUTO = None
 
 
-SHORT_FLOPS = 50_000_000_000
+LOCAL_FLOPS = 50_000_000_000
 
 def fast(*dims, dtype=F32):
     return pltpu.VMEM(dims, dtype)
@@ -72,9 +73,13 @@
     return copy
 
 
-def pieces(width, count):
+def piece(width, count, index):
     size = width // count
-    return [pl.ds(i * size, size) for i in range(count)]
+    return pl.ds(pl.multiple_of(index * size, size), size)
+
+
+def over(count, body):
+    lax.fori_loop(0, count, lambda index, carry: body(index) or carry, 0)
 
 
 def rim_kernel(seg, sek, sev, lig, lik, liv, after, out, tails, held, sems):
@@ -92,21 +97,32 @@
     out[...] = held[...].astype(BF16)
 
 
-CHUNK = 8
+CHUNK = 4
 
 
 def states_kernel(key_hbm, value_hbm, feature_hbm, rate_hbm, kept_hbm, sent_hbm, key, value, feature, rate, kept, sent, wide, fresh, sems, outs):
     width = key.shape[1]
     chunks = width // (CHUNK * LANES)
-    spans = pieces(width, chunks)
+
+    def large(index):
+        span = piece(width, chunks, index)
+        return [
+            pltpu.make_async_copy(key_hbm.at[:, span], key.at[:, span], sems.at[2 + 2 * index]),
+            pltpu.make_async_copy(value_hbm.at[:, span], value.at[:, span], sems.at[3 + 2 * index]),
+        ]
+
+    def leaving(index):
+        span = piece(width, chunks, index)
+        owners = pl.ds(index * (CHUNK // 2), CHUNK // 2)
+        return [
+            pltpu.make_async_copy(sent.at[owners], sent_hbm.at[owners], outs.at[2 * index]),
+            pltpu.make_async_copy(kept.at[:, :, span], kept_hbm.at[:, :, span], outs.at[2 * index + 1]),
+        ]
+
     small = [started(feature_hbm, feature, sems.at[0]), started(rate_hbm, rate, sems.at[1])]
-    large = [
-        (
-            started(key_hbm.at[:, span], key.at[:, span], sems.at[2 + 2 * i]),
-            started(value_hbm.at[:, span], value.at[:, span], sems.at[3 + 2 * i]),
-        )
-        for i, span in enumerate(spans)
-    ]
+    for index in range(chunks):
+        for copy in large(index):
+            copy.start()
     for copy in small:
         copy.wait()
 
@@ -120,15 +136,15 @@
         )
 
     wide[:, :, 0:8] = jnp.zeros((2, 3, 8, LANES), F32)
-    leaving = []
-    for index in range(chunks):
-        for copy in large[index]:
+
+    def chunk(index):
+        for copy in large(index):
             copy.wait()
         decays = []
         for part in range(CHUNK):
             block = index * CHUNK + part
-            lanes = pl.ds(block * LANES, LANES)
-            owner = block // 2
+            lanes = lanes_at(block)
+            owner = index * (CHUNK // 2) + part // 2
             half = slice((part % 2) * LANES, (part % 2 + 1) * LANES)
             slot = part % 2
             u = featurized(key, 1, lanes, slot) * featurized(value, 2, lanes, slot)
@@ -138,28 +154,27 @@
             sent[owner, 18:20, half] = wide[slot, 2, 8:10]
             sent[owner, 20:22, half] = wide[slot, 1, ROWS + 6 : ROWS + 8]
             sent[owner, 22:24, half] = wide[slot, 2, ROWS + 6 : ROWS + 8]
-            decays.append(jnp.exp(-rate[:, lanes]))
-
-        def group(g, states):
+            decays.append([jnp.exp(-times * rate[:, lanes]) for times in (1.0, 2.0, 4.0)])
+        states = [jnp.zeros((MODES, LANES), F32)] * CHUNK
+        for t in range(0, ROWS, 4):
             for part in range(CHUNK):
-                kept[g, :, pl.ds((index * CHUNK + part) * LANES, LANES)] = states[part]
-            states = list(states)
-            for t in range(STEP):
-                for part in range(CHUNK):
-                    row = fresh[part, pl.ds(g * STEP + t, 1), :]
-                    states[part] = decays[part] * states[part] + row
-            return tuple(states)
-
-        zero = jnp.zeros((MODES, LANES), F32)
-        states = lax.fori_loop(0, GROUPS, group, (zero,) * CHUNK)
+                if t % STEP == 0:
+                    kept[t // STEP, :, lanes_at(index * CHUNK + part)] = states[part]
+                row = [fresh[part, t + i : t + i + 1, :] for i in range(4)]
+                one, two, four = decays[part]
+                first = one * row[0] + row[1]
+                second = one * row[2] + row[3]
+                states[part] = four * states[part] + (two * first + second)
         for part in range(CHUNK):
             half = slice((part % 2) * LANES, (part % 2 + 1) * LANES)
-            sent[(index * CHUNK + part) // 2, 0:MODES, half] = states[part]
-        owners = pl.ds(index * CHUNK // 2, CHUNK // 2)
-        leaving.append(started(sent.at[owners], sent_hbm.at[owners], outs.at[2 * index]))
-        leaving.append(started(kept.at[:, :, spans[index]], kept_hbm.at[:, :, spans[index]], outs.at[2 * index + 1]))
-    for copy in leaving:
-        copy.wait()
+            sent[index * (CHUNK // 2) + part // 2, 0:MODES, half] = states[part]
+        for copy in leaving(index):
+            copy.start()
+
+    over(chunks, chunk)
+    for index in range(chunks):
+        for copy in leaving(index):
+            copy.wait()
 
 
 def first_two(taps, own, before):
@@ -176,16 +191,19 @@
     return ((k0 * v0).astype(BF16).astype(F32), (k1 * v1).astype(BF16).astype(F32))
 
 
-def owned(feature, rate, chips):
-    width = 2 * LANES
+def owned_lanes(chips, width):
     me = lax.axis_index("core") * chips + lax.axis_index("chip")
-    lanes = pl.ds(pl.multiple_of(me * width, width), width)
+    return pl.ds(pl.multiple_of(me * width, width), width)
+
+
+def taps_of(feature):
+    return [[feature[j, s : s + 1] for j in range(3)] for s in (1, 2)]
+
+
+def group_kernel(chips, came, feature, rate, sent_hbm, full_hbm, sent, full, sems):
+    lanes = owned_lanes(chips, came.shape[2])
     taps = [[feature[j, s : s + 1, lanes] for j in range(3)] for s in (1, 2)]
-    return taps, rate[:, lanes]
-
-
-def group_kernel(chips, came, feature, rate, sent_hbm, full_hbm, sent, full, sems):
-    taps, pace = owned(feature, rate, chips)
+    pace = rate[:, lanes]
     e_block = jnp.exp(-float(ROWS) * pace)
     e_first = jnp.exp(-float(ROWS - 1) * pace)
     e_second = jnp.exp(-float(ROWS - 2) * pace)
@@ -205,9 +223,13 @@
         copy.wait()
 
 
-def carry_kernel(chips, came, full_hbm, feature, rate, out_hbm, full, out, sems):
+def carry_kernel(chips, came, full_hbm, feature_hbm, rate, out_hbm, full, out, feature, sems):
+    lanes = owned_lanes(chips, came.shape[2])
     arriving = started(full_hbm, full, sems.at[0])
-    taps, pace = owned(feature, rate, chips)
+    tapping = started(feature_hbm.at[:, :, lanes], feature, sems.at[2])
+    pace = rate[:, lanes]
+    tapping.wait()
+    taps = taps_of(feature)
     me = lax.axis_index(FAR)
     peers = full.shape[0]
     span = float(ROWS * peers)
@@ -239,21 +261,45 @@
 
 
 def reach_kernel(rate, weight, out):
-    place = (lax.broadcasted_iota(jnp.int32, (STEP, LANES), 0) + 1).astype(F32)
-
-    def block(index, carry):
+    place = (lax.broadcasted_iota(jnp.int32, (HALF, LANES), 0) + 1).astype(F32)
+
+    def block(index):
         lanes = lanes_at(index)
-        total = jnp.zeros((STEP, LANES), F32)
         for m in range(MODES):
-            tap = weight[m : m + 1, lanes] * jnp.exp(-place * rate[m : m + 1, lanes])
-            out[m, :, lanes] = tap
-            total = total + tap
-        out[MODES, :, lanes] = total
-        now = jnp.sum(weight[:, lanes], axis=0, keepdims=True)
-        out[MODES, STEP - 1 : STEP, lanes] = now
-        return carry
-
-    lax.fori_loop(0, rate.shape[1] // LANES, block, 0)
+            out[m, :, lanes] = weight[m : m + 1, lanes] * jnp.exp(-place * rate[m : m + 1, lanes])
+
+    over(rate.shape[1] // LANES, block)
+
+
+def fill_lags(reach, rate, lags):
+    def block(index):
+        lanes = lanes_at(index)
+        pace = rate[:, lanes]
+        far = jnp.exp(-float(HALF) * pace)
+        back = jnp.exp(pace)
+        low = jnp.zeros((HALF, LANES), F32)
+        high = low
+        now = jnp.zeros((1, LANES), F32)
+        for m in range(MODES):
+            tap = reach[m, :, lanes]
+            low = low + tap
+            high = high + tap * far[m : m + 1]
+            now = now + tap[0:1] * back[m : m + 1]
+        lags[0:HALF, lanes] = low
+        lags[HALF:STEP, lanes] = high
+        lags[STEP - 1 : STEP, lanes] = now
+
+    over(rate.shape[1] // LANES, block)
+
+
+def add_modes(low, high, reach, rows, slot, lanes):
+    for m in range(MODES):
+        near = reach[m, :, lanes]
+        far = near * rows[slot, GROUPS * MODES + m : GROUPS * MODES + m + 1]
+        for g in range(GROUPS):
+            state = rows[slot, g * MODES + m : g * MODES + m + 1]
+            low[g] = low[g] + near * state
+            high[g] = high[g] + far * state
 
 
 SHORT_PIECES = 4
@@ -263,16 +309,26 @@
     gate_hbm, key_hbm, value_hbm, rim_hbm, feature_hbm, taps_hbm, out_hbm, gate, key, value, rim, feature, taps, out, kw, vw, gw, uw, sems, outs
 ):
     width = key.shape[1]
-    spans = pieces(width, SHORT_PIECES)
+
+    def large(index):
+        span = piece(width, SHORT_PIECES, index)
+        return [
+            pltpu.make_async_copy(a.at[:, span], b.at[:, span], sems.at[3 + 3 * index + j])
+            for j, (a, b) in enumerate(((gate_hbm, gate), (key_hbm, key), (value_hbm, value)))
+        ]
+
+    def leaving(index):
+        span = piece(width, SHORT_PIECES, index)
+        return pltpu.make_async_copy(out.at[:, span], out_hbm.at[:, span], outs.at[index])
+
     small = [
         started(rim_hbm, rim, sems.at[0]),
         started(feature_hbm, feature, sems.at[1]),
         started(taps_hbm, taps, sems.at[2]),
     ]
-    large = [
-        [started(a.at[:, span], b.at[:, span], sems.at[3 + 3 * i + j]) for j, (a, b) in enumerate(((gate_hbm, gate), (key_hbm, key), (value_hbm, value)))]
-        for i, span in enumerate(spans)
-    ]
+    for index in range(SHORT_PIECES):
+        for copy in large(index):
+            copy.start()
     for slot in range(2):
         kw[slot, 0:8] = jnp.zeros((8, LANES), F32)
         vw[slot, 0:8] = jnp.zeros((8, LANES), F32)
@@ -306,47 +362,51 @@
         out[:, lanes] = (feat(gw, 0, 16, ROWS) * mixed).astype(BF16)
 
     each = width // SHORT_PIECES // LANES // 2
-    leaving = []
-    for i, span in enumerate(spans):
-        for copy in large[i]:
+
+    def some(index):
+        for copy in large(index):
             copy.wait()
 
-        def pair(index, carry):
+        def pair(inner):
             for slot in range(2):
-                one((i * each + index) * 2 + slot, slot)
-            return carry
-
-        lax.fori_loop(0, each, pair, 0)
-        leaving.append(started(out.at[:, span], out_hbm.at[:, span], outs.at[i]))
-    for copy in leaving:
-        copy.wait()
+                one((index * each + inner) * 2 + slot, slot)
+
+        over(each, pair)
+        leaving(index).start()
+
+    over(SHORT_PIECES, some)
+    for index in range(SHORT_PIECES):
+        leaving(index).wait()
 
 
 LOCAL_PIECES = 4
 
 
 def local_kernel(
-    gate_hbm, key_hbm, value_hbm, rim_hbm, feature_hbm, skip_hbm, kept_hbm, reach, rate, out_hbm, out, gate, key, value, rim, feature, skip, kept, kw, vw, gw, uw, sems, outs
+    gate_hbm, key_hbm, value_hbm, rim_hbm, feature_hbm, skip_hbm, kept_hbm, reach, rate, out, gate, key, value, rim, feature, skip, lags, kept, kw, vw, gw, uw, rows, sems
 ):
     width = key.shape[1]
-    spans = pieces(width, LOCAL_PIECES)
+
+    def large(index):
+        span = piece(width, LOCAL_PIECES, index)
+        pairs = ((gate_hbm, gate), (key_hbm, key), (value_hbm, value))
+        return [
+            pltpu.make_async_copy(a.at[:, span], b.at[:, span], sems.at[4 + 4 * index + j]) for j, (a, b) in enumerate(pairs)
+        ] + [pltpu.make_async_copy(kept_hbm.at[:, :, span], kept.at[:, :, span], sems.at[7 + 4 * index])]
+
     small = [
         started(rim_hbm, rim, sems.at[0]),
         started(feature_hbm, feature, sems.at[1]),
         started(skip_hbm, skip, sems.at[2]),
     ]
-    large = [
-        [
-            started(a.at[:, span], b.at[:, span], sems.at[3 + 4 * i + j])
-            for j, (a, b) in enumerate(((gate_hbm, gate), (key_hbm, key), (value_hbm, value)))
-        ]
-        + [started(kept_hbm.at[:, :, span], kept.at[:, :, span], sems.at[6 + 4 * i])]
-        for i, span in enumerate(spans)
-    ]
+    for index in range(LOCAL_PIECES):
+        for copy in large(index):
+            copy.start()
     for w in (kw, vw, gw, uw):
         for slot in range(2):
             w[slot, 0:16] = jnp.zeros((16, LANES), F32)
     place = lax.broadcasted_iota(jnp.int32, (STEP, LANES), 0)
+    fill_lags(reach, rate, lags)
     for copy in small:
         copy.wait()
 
@@ -369,82 +429,80 @@
         pace = rate[:, lanes]
         jump = jnp.exp(-float(STEP) * pace)
         state = uw[slot, 16:17] * jnp.exp(-float(STEP - 1) * pace) + uw[slot, 17:18] * jnp.exp(-float(STEP - 2) * pace)
+        rows[slot, 0:MODES] = jnp.zeros((MODES, LANES), F32)
         for g in range(1, GROUPS):
-            out[2 * ROWS + g * MODES : 2 * ROWS + (g + 1) * MODES, lanes] = kept[g, :, lanes] + state
+            rows[slot, g * MODES : (g + 1) * MODES] = kept[g, :, lanes] + state
             state = state * jump
-        now = reach[MODES, STEP - 1 : STEP, lanes] + skip[:, lanes]
+        rows[slot, GROUPS * MODES : (GROUPS + 1) * MODES] = jnp.exp(-float(HALF) * pace)
+        now = lags[STEP - 1 : STEP, lanes] + skip[:, lanes]
         low, high = [], []
         for g in range(GROUPS):
             start = 16 + g * STEP
-            low.append(now * uw[slot, start : start + 8])
-            high.append(now * uw[slot, start + 8 : start + STEP])
+            low.append(now * uw[slot, start : start + HALF])
+            high.append(now * uw[slot, start + HALF : start + STEP])
         for lag in range(1, STEP):
-            tap = jnp.where(place >= lag, reach[MODES, lag - 1 : lag, lanes], 0.0)
+            tap = jnp.where(place >= lag, lags[lag - 1 : lag, lanes], 0.0)
             for g in range(GROUPS):
                 start = 16 + g * STEP - lag
-                if lag < 8:
-                    low[g] = low[g] + tap[0:8] * uw[slot, start : start + 8]
-                high[g] = high[g] + tap[8:STEP] * uw[slot, start + 8 : start + STEP]
+                if lag < HALF:
+                    low[g] = low[g] + tap[0:HALF] * uw[slot, start : start + HALF]
+                high[g] = high[g] + tap[HALF:STEP] * uw[slot, start + HALF : start + STEP]
+        add_modes(low, high, reach, rows, slot, lanes)
         for g in range(GROUPS):
-            out[g * STEP : g * STEP + 8, lanes] = low[g]
-            out[g * STEP + 8 : (g + 1) * STEP, lanes] = high[g]
+            out[g * STEP : g * STEP + HALF, lanes] = low[g]
+            out[g * STEP + HALF : (g + 1) * STEP, lanes] = high[g]
 
     each = width // LOCAL_PIECES // LANES // 2
-    leaving = []
-    for i, span in enumerate(spans):
-        for copy in large[i]:
+    for index in range(LOCAL_PIECES):
+        for copy in large(index):
             copy.wait()
 
-        def pair(index, carry):
+        def pair(inner):
             for slot in range(2):
-                one((i * each + index) * 2 + slot, slot)
-            return carry
-
-        lax.fori_loop(0, each, pair, 0)
-        leaving.append(started(out.at[:, span], out_hbm.at[:, span], outs.at[i]))
-    for copy in leaving:
-        copy.wait()
+                one((index * each + inner) * 2 + slot, slot)
+
+        over(each, pair)
 
 
 FINISH_PIECES = 4
 
 
-def finish_kernel(came, local_hbm, reach, rate, out_hbm, local, out, rows, sems, outs):
+def finish_kernel(came, local, reach, rate, out_hbm, out, rows, outs):
     width = rate.shape[1]
-    spans = pieces(width, FINISH_PIECES)
-    arriving = [started(local_hbm.at[:, span], local.at[:, span], sems.at[i]) for i, span in enumerate(spans)]
+
+    def leaving(index):
+        span = piece(width, FINISH_PIECES, index)
+        return pltpu.make_async_copy(out.at[:, span], out_hbm.at[:, span], outs.at[index])
+
     each = width // FINISH_PIECES // LANES // 2
 
     def one(owner, slot):
         lanes = lanes_at(owner * 2 + slot)
         state = came[owner, :, slot * LANES : (slot + 1) * LANES]
-        rows[slot, 0:MODES] = state
-        jump = jnp.exp(-float(STEP) * rate[:, lanes])
-        for g in range(1, GROUPS):
+        pace = rate[:, lanes]
+        jump = jnp.exp(-float(STEP) * pace)
+        for g in range(GROUPS):
+            rows[slot, g * MODES : (g + 1) * MODES] = state
             state = state * jump
-            rows[slot, g * MODES : (g + 1) * MODES] = state + local[2 * ROWS + g * MODES : 2 * ROWS + (g + 1) * MODES, lanes]
-        totals = [local[g * STEP : (g + 1) * STEP, lanes] for g in range(GROUPS)]
-        for m in range(MODES):
-            tap = reach[m, :, lanes]
-            for g in range(GROUPS):
-                totals[g] = totals[g] + tap * rows[slot, g * MODES + m : g * MODES + m + 1]
+        rows[slot, GROUPS * MODES : (GROUPS + 1) * MODES] = jnp.exp(-float(HALF) * pace)
+        low = [local[g * STEP : g * STEP + HALF, lanes] for g in range(GROUPS)]
+        high = [local[g * STEP + HALF : (g + 1) * STEP, lanes] for g in range(GROUPS)]
+        add_modes(low, high, reach, rows, slot, lanes)
         for g in range(GROUPS):
-            total = local[ROWS + g * STEP : ROWS + (g + 1) * STEP, lanes] * totals[g]
+            total = local[ROWS + g * STEP : ROWS + (g + 1) * STEP, lanes] * jnp.concatenate([low[g], high[g]], axis=0)
             out[g * STEP : (g + 1) * STEP, lanes] = total.astype(BF16)
 
-    leaving = []
-    for i, span in enumerate(spans):
-
-        def pair(index, carry):
+    def some(index):
+        def pair(inner):
             for slot in range(2):
-                one(i * each + index, slot)
-            return carry
-
-        arriving[i].wait()
-        lax.fori_loop(0, each, pair, 0)
-        leaving.append(started(out.at[:, span], out_hbm.at[:, span], outs.at[i]))
-    for copy in leaving:
-        copy.wait()
+                one(index * each + inner, slot)
+
+        over(each, pair)
+        leaving(index).start()
+
+    over(FINISH_PIECES, some)
+    for index in range(FINISH_PIECES):
+        leaving(index).wait()
 
 
 def shards(
@@ -506,7 +564,7 @@
     )(se_gate, se_key, se_value, li_gate, li_key, li_value, kept)
     weight = li_residue * jnp.sqrt(-jnp.expm1(-2.0 * li_rate))
     reach = call(
-        reach_kernel, "reach", [AUTO] * 2, [(fast(MODES + 1, STEP, width), AUTO)], [], 3000000, 2000000
+        reach_kernel, "reach", [AUTO] * 2, [(fast(MODES, HALF, width), AUTO)], [], 3000000, 2000000
     )(li_rate, weight)
     came, reach = lax.optimization_barrier((came, reach))
 
@@ -523,6 +581,44 @@
     groups = swap(group, FAR)
     count = lax.axis_size(PART)
     halo = lax.ppermute(rim, PART, [(i, i + 1) for i in range(count - 1)])
+    local = call(
+        local_kernel,
+        "local",
+        [HBM] * 7 + [AUTO] * 2,
+        [(fast(2 * ROWS, width), AUTO)],
+        [
+            stream,
+            stream,
+            stream,
+            rim_room,
+            feature_room,
+            room(1, width),
+            room(STEP, width),
+            room(GROUPS, MODES, width),
+            padded,
+            padded,
+            padded,
+            padded,
+            room(2, (GROUPS + 1) * MODES, LANES),
+            dma((4 + 4 * LOCAL_PIECES,)),
+        ],
+        LOCAL_FLOPS,
+        3000000,
+    )(li_gate, li_key, li_value, halo, li_feature, li_skip.reshape(1, width), kept, reach, li_rate)
+
+    groups, local = lax.optimization_barrier((groups, local))
+
+    states = call(
+        functools.partial(carry_kernel, chips),
+        "carry",
+        [AUTO, HBM, HBM, AUTO],
+        [(slow(near, MODES, part), HBM)],
+        [room(near, MODES, part), room(near, MODES, part), room(3, 3, part), dma((3,))],
+        500000,
+        500000,
+    )(groups, full, li_feature, li_rate)
+
+    back = swap(states, NEAR)
     se_out = call(
         short_kernel,
         "short",
@@ -543,53 +639,15 @@
             dma((3 + 3 * SHORT_PIECES,)),
             dma((SHORT_PIECES,)),
         ],
-        SHORT_FLOPS,
+        12000000,
         2000000,
     )(se_gate, se_key, se_value, halo, se_feature, se_filter)
-    groups, se_out = lax.optimization_barrier((groups, se_out))
-
-    states = call(
-        functools.partial(carry_kernel, chips),
-        "carry",
-        [AUTO, HBM, AUTO, AUTO],
-        [(slow(near, MODES, part), HBM)],
-        [room(near, MODES, part), room(near, MODES, part), dma((2,))],
-        500000,
-        500000,
-    )(groups, full, li_feature, li_rate)
-
-    back = swap(states, NEAR)
-    local = call(
-        local_kernel,
-        "local",
-        [HBM] * 7 + [AUTO] * 2,
-        [(slow(3 * ROWS, width), HBM)],
-        [
-            room(3 * ROWS, width),
-            stream,
-            stream,
-            stream,
-            rim_room,
-            feature_room,
-            room(1, width),
-            room(GROUPS, MODES, width),
-            padded,
-            padded,
-            padded,
-            padded,
-            dma((3 + 4 * LOCAL_PIECES,)),
-            dma((LOCAL_PIECES,)),
-        ],
-        12000000,
-        3000000,
-    )(li_gate, li_key, li_value, halo, li_feature, li_skip.reshape(1, width), kept, reach, li_rate)
-
     li_out = call(
         finish_kernel,
         "finish",
-        [AUTO, HBM, AUTO, AUTO],
+        [AUTO] * 4,
         [(slow(ROWS, width, dtype=BF16), HBM)],
-        [room(3 * ROWS, width), stream, room(2, GROUPS * MODES, LANES), dma((FINISH_PIECES,)), dma((FINISH_PIECES,))],
+        [stream, room(2, (GROUPS + 1) * MODES, LANES), dma((FINISH_PIECES,))],
         10000000,
         5000000,
     )(back, local, reach, li_rate)

time: 50.4 us -> 48.9 us (0.970)
  Pallas kernels: 20.4 us -> 18.9 us
    pallas_call x8, Pallas kernels: 20.4 us -> 18.9 us  [outer(): inner(*[pltpu.with_memory_space_constraint(v, pltpu.HBM) if spec is HBM e...]
  transfers between devices with their start and end apart: 4 -> 4, of which waited for: 3 -> 3; matrix products, arithmetic and copies ran while one was open for 0% -> 0% of each run, Pallas kernels for 22% -> 23%
where the time goes in v1:
time: 48.9 us; the launch traced here: 48.4 us
  starting transfers between devices  23.7 us (48%)
  Pallas kernels  18.9 us (39%)
  waiting for transfers between devices  4.32 us (9%)
  between operations  0.75 us (2%)
  local copies, waits for them, and re-layouts  0.65 us (1%)
    all_to_all x3, starting transfers between devices, shards(): lax.all_to_all(value, axis, split_axis=0, concat_axis=0, tiled=True)  20.4 us
    pallas_call x8, Pallas kernels, outer(): inner(*[pltpu.with_memory_space_constraint(v, pltpu.HBM) if spec is HBM e...  18.9 us
    all_to_all x3, waiting for transfers between devices, shards(): lax.all_to_all(value, axis, split_axis=0, concat_axis=0, tiled=True)  4.32 us
    ppermute x1, starting transfers between devices, shards(): halo = lax.ppermute(rim, PART, [(i, i + 1) for i in range(count - 1)])  3.28 us
  transfers between devices with their start and end apart: 4, of which 3 were waited for; matrix products, arithmetic and copies ran while one was open for 0% of the time, Pallas kernels for 23%

profile of v1, /device:TPU:1, one launch (start us, length us, event | category | flops | bytes accessed | tf_op | source)
XLA Modules:
  0.0 48.4 jit_solution(2278840358792883294)
XLA Ops:
  0.6 3.9 %states.1 = (f32[8,16,2048]{2,1,0:T(8,128)}, f32[8,24,256]{2,1,0:T(8,128)}) custom-call(bf16[128,2048]{1,0:T(8,128)(2,1)} %key_hbm.5, bf16[128,2048]{1,0:T(8,128)(2,1)} %value_hbm.5, f32[3,3,2048]{2,1,0:T(4,128)} %feature_hbm.7, f32[16,2048]{1,0:T(8,128)} %rate.9), custom_call_target="tpu_custom_call" | custom-call | flops 12000000 | bytes 3000000 | tf_op jit(solution)/shard_map/states/pallas_call | solution.py:59
  4.5 10.2 %all-to-all-start = ((f32[8,24,256]{2,1,0:T(8,128)}), f32[8,24,256]{2,1,0:T(8,128)S(1)}, u32[]{:S(2)}, u32[]{:S(2)}) async-start(f32[8,24,256]{2,1,0:T(8,128)} %get-tuple-element.11), calls=%async_computation | async-start | bytes 393216 | tf_op jit(solution)/shard_map/all_to_all | solution.py:527
  14.7 0.0 copy-start
  14.7 0.0 copy-start.2
  14.7 1.1 %rim.1 = bf16[32,2048]{1,0:T(8,128)(2,1)S(1)} custom-call(bf16[128,2048]{1,0:T(8,128)(2,1)} %gate_hbm.2, bf16[128,2048]{1,0:T(8,128)(2,1)} %key_hbm.4, bf16[128,2048]{1,0:T(8,128)(2,1)} %value_hbm.4, bf16[128,2048]{1,0:T(8,128)(2,1)} %gate_hbm.3, bf16[128,2048]{1,0:T(8,128)(2,1)} %key_hbm.5, bf16[128,2048]{1,0:T(8,128)(2,1)} %value_hbm.5, ...), custom_call_target="tpu_custom_call" | custom-call | flops 1000000 | bytes 500000 | tf_op jit(solution)/shard_map/rim/pallas_call | solution.py:59
  15.9 3.3 %collective-permute-start = (bf16[32,2048]{1,0:T(8,128)(2,1)S(1)}, bf16[32,2048]{1,0:T(8,128)(2,1)S(1)}, u32[]{:S(2)}, u32[]{:S(2)}) collective-permute-start(bf16[32,2048]{1,0:T(8,128)(2,1)S(1)} %rim.1), channel_id=1, source_target_pairs={{0,1},{1,2},{2,3},{3,4},{4,5},{5,6},{6,7},{7,8},{8,9},{9,10},{10,1... | collective-permute-start | bytes 393224 | tf_op jit(solution)/shard_map/ppermute | solution.py:583
  19.2 0.0 copy-done
  19.2 0.0 copy-done.2
  19.2 0.1 sqrt_multiply_fusion.weight
  19.3 0.3 reach.1
  19.6 1.0 %all-to-all-done.came = f32[8,24,256]{2,1,0:T(8,128)S(1)} async-done(((f32[8,24,256]{2,1,0:T(8,128)}), f32[8,24,256]{2,1,0:T(8,128)S(1)}, u32[]{:S(2)}, u32[]{:S(2)}) %all-to-all-start) | async-done | bytes 196640 | tf_op jit(solution)/shard_map/all_to_all | solution.py:527
  20.6 0.0 copy-done.1
  20.6 0.9 %group.1 = (bf16[16,24,256]{2,1,0:T(8,128)(2,1)}, f32[8,16,256]{2,1,0:T(8,128)}) custom-call(f32[8,24,256]{2,1,0:T(8,128)S(1)} %all-to-all-done.came, f32[3,3,2048]{2,1,0:T(4,128)S(1)} %copy-done.1, f32[16,2048]{1,0:T(8,128)S(1)} %copy-done), custom_call_target="tpu_custom_call" | custom-call | flops 500000 | bytes 500000 | tf_op jit(solution)/shard_map/group/pallas_call | solution.py:59
  21.6 4.0 %all-to-all-start.1 = ((bf16[16,24,256]{2,1,0:T(8,128)(2,1)}), bf16[16,24,256]{2,1,0:T(8,128)(2,1)S(1)}, u32[]{:S(2)}, u32[]{:S(2)}) async-start(bf16[16,24,256]{2,1,0:T(8,128)(2,1)} %get-tuple-element.13), calls=%async_computation.1 | async-start | bytes 393216 | tf_op jit(solution)/shard_map/all_to_all | solution.py:527
  25.6 0.0 collective-permute-done.rim_hbm
  25.6 0.0 copy-start.3
  25.6 0.6 %copy-done.3 = bf16[32,2048]{1,0:T(8,128)(2,1)} copy-done((bf16[32,2048]{1,0:T(8,128)(2,1)}, bf16[32,2048]{1,0:T(8,128)(2,1)S(1)}, u32[]{:S(2)}) %copy-start.3) | copy-done | bytes 131096
  26.2 4.9 %local.1 = f32[256,2048]{1,0:T(8,128)S(1)} custom-call(bf16[128,2048]{1,0:T(8,128)(2,1)} %gate_hbm.3, bf16[128,2048]{1,0:T(8,128)(2,1)} %key_hbm.5, bf16[128,2048]{1,0:T(8,128)(2,1)} %value_hbm.5, bf16[32,2048]{1,0:T(8,128)(2,1)} %copy-done.3, f32[3,3,2048]{2,1,0:T(4,128)} %feature_hbm.7, f32[1,2048]{1,0:T(1,128)} %bitcast.1, ...), custom_call_target="tpu_custom_call" | custom-call | flops 49999998976 | bytes 3000000 | tf_op jit(solution)/shard_map/local/pallas_call | solution.py:59
  31.1 1.9 %all-to-all-done.1.came = bf16[16,24,256]{2,1,0:T(8,128)(2,1)S(1)} async-done(((bf16[16,24,256]{2,1,0:T(8,128)(2,1)}), bf16[16,24,256]{2,1,0:T(8,128)(2,1)S(1)}, u32[]{:S(2)}, u32[]{:S(2)}) %all-to-all-start.1) | async-done | bytes 196640 | tf_op jit(solution)/shard_map/all_to_all | solution.py:527
  33.1 1.7 %carry.1 = f32[8,16,256]{2,1,0:T(8,128)} custom-call(bf16[16,24,256]{2,1,0:T(8,128)(2,1)S(1)} %all-to-all-done.1.came, f32[8,16,256]{2,1,0:T(8,128)} %get-tuple-element.16.full_hbm, f32[3,3,2048]{2,1,0:T(4,128)} %feature_hbm.7, f32[16,2048]{1,0:T(8,128)S(1)} %copy-done), custom_call_target="tpu_custom_call" | custom-call | flops 500000 | bytes 500000 | tf_op jit(solution)/shard_map/carry/pallas_call | solution.py:59
  34.8 6.2 %all-to-all-start.2 = ((f32[8,16,256]{2,1,0:T(8,128)}), f32[8,16,256]{2,1,0:T(8,128)S(1)}, u32[]{:S(2)}, u32[]{:S(2)}) async-start(f32[8,16,256]{2,1,0:T(8,128)} %carry.1), calls=%async_computation.2 | async-start | bytes 262144 | tf_op jit(solution)/shard_map/all_to_all | solution.py:527
  41.0 3.8 %short.1 = bf16[128,2048]{1,0:T(8,128)(2,1)} custom-call(bf16[128,2048]{1,0:T(8,128)(2,1)} %gate_hbm.2, bf16[128,2048]{1,0:T(8,128)(2,1)} %key_hbm.4, bf16[128,2048]{1,0:T(8,128)(2,1)} %value_hbm.4, bf16[32,2048]{1,0:T(8,128)(2,1)} %copy-done.3, f32[3,3,2048]{2,1,0:T(4,128)} %feature_hbm.5, f32[7,2048]{1,0:T(8,128)} %taps_hbm.1), custom_call_target="tpu_custom_call" | custom-call | flops 12000000 | bytes 2000000 | tf_op jit(solution)/shard_map/short/pallas_call | solution.py:59
  44.8 1.4 %all-to-all-done.2.came = f32[8,16,256]{2,1,0:T(8,128)S(1)} async-done(((f32[8,16,256]{2,1,0:T(8,128)}), f32[8,16,256]{2,1,0:T(8,128)S(1)}, u32[]{:S(2)}, u32[]{:S(2)}) %all-to-all-start.2) | async-done | bytes 131104 | tf_op jit(solution)/shard_map/all_to_all | solution.py:527
  46.2 2.2 %finish.1 = bf16[128,2048]{1,0:T(8,128)(2,1)} custom-call(f32[8,16,256]{2,1,0:T(8,128)S(1)} %all-to-all-done.2.came, f32[256,2048]{1,0:T(8,128)S(1)} %local.1, f32[16,8,2048]{2,1,0:T(8,128)S(1)} %reach.1, f32[16,2048]{1,0:T(8,128)S(1)} %copy-done), custom_call_target="tpu_custom_call" | custom-call | flops 10000000 | bytes 5000000 | tf_op jit(solution)/shard_map/finish/pallas_call | solution.py:59
  (1 shorter events, 0.0 us)
Async XLA Ops:
  4.5 16.1 %all-to-all-start = ((f32[8,24,256]{2,1,0:T(8,128)}), f32[8,24,256]{2,1,0:T(8,128)S(1)}, u32[]{:S(2)}, u32[]{:S(2)}) async-start(f32[8,24,256]{2,1,0:T(8,128)} %get-tuple-element.11), calls=%async_computation | async-start | bytes 393216 | tf_op jit(solution)/shard_map/all_to_all | solution.py:527
  14.7 4.4 %copy-start = (f32[16,2048]{1,0:T(8,128)S(1)}, f32[16,2048]{1,0:T(8,128)}, u32[]{:S(2)}) copy-start(f32[16,2048]{1,0:T(8,128)} %rate.9) | copy-start | bytes 393220
  14.7 4.5 %copy-start.2 = (f32[16,2048]{1,0:T(8,128)S(1)}, f32[16,2048]{1,0:T(8,128)}, u32[]{:S(2)}) copy-start(f32[16,2048]{1,0:T(8,128)} %param.21) | copy-start | bytes 393220
  14.7 5.9 %copy-start.1 = (f32[3,3,2048]{2,1,0:T(4,128)S(1)}, f32[3,3,2048]{2,1,0:T(4,128)}, u32[]{:S(2)}) copy-start(f32[3,3,2048]{2,1,0:T(4,128)} %feature_hbm.7) | copy-start | bytes 221188
  15.9 9.7 %collective-permute-start = (bf16[32,2048]{1,0:T(8,128)(2,1)S(1)}, bf16[32,2048]{1,0:T(8,128)(2,1)S(1)}, u32[]{:S(2)}, u32[]{:S(2)}) collective-permute-start(bf16[32,2048]{1,0:T(8,128)(2,1)S(1)} %rim.1), channel_id=1, source_target_pairs={{0,1},{1,2},{2,3},{3,4},{4,5},{5,6},{6,7},{7,8},{8,9},{9,10},{10,1... | collective-permute-start | bytes 393224 | tf_op jit(solution)/shard_map/ppermute | solution.py:583
  21.6 11.5 %all-to-all-start.1 = ((bf16[16,24,256]{2,1,0:T(8,128)(2,1)}), bf16[16,24,256]{2,1,0:T(8,128)(2,1)S(1)}, u32[]{:S(2)}, u32[]{:S(2)}) async-start(bf16[16,24,256]{2,1,0:T(8,128)(2,1)} %get-tuple-element.13), calls=%async_computation.1 | async-start | bytes 393216 | tf_op jit(solution)/shard_map/all_to_all | solution.py:527
  25.6 0.6 %copy-start.3 = (bf16[32,2048]{1,0:T(8,128)(2,1)}, bf16[32,2048]{1,0:T(8,128)(2,1)S(1)}, u32[]{:S(2)}) copy-start(bf16[32,2048]{1,0:T(8,128)(2,1)S(1)} %collective-permute-done.rim_hbm) | copy-start | bytes 393220
  34.8 11.4 %all-to-all-start.2 = ((f32[8,16,256]{2,1,0:T(8,128)}), f32[8,16,256]{2,1,0:T(8,128)S(1)}, u32[]{:S(2)}, u32[]{:S(2)}) async-start(f32[8,16,256]{2,1,0:T(8,128)} %carry.1), calls=%async_computation.2 | async-start | bytes 262144 | tf_op jit(solution)/shard_map/all_to_all | solution.py:527

commit v2 on v1

--- a/solution.py
+++ b/solution.py
@@ -82,25 +82,27 @@
     lax.fori_loop(0, count, lambda index, carry: body(index) or carry, 0)
 
 
-def rim_kernel(seg, sek, sev, lig, lik, liv, after, out, tails, held, sems):
-    del after
-    copies = [started(ref.at[ROWS - 16 : ROWS], tails.at[i], sems.at[i]) for i, ref in enumerate((seg, sek, sev, lig, lik, liv))]
-    held[24:32] = jnp.zeros_like(held[24:32])
-    for copy in copies:
-        copy.wait()
+def fill_rim(tails, key, value, held, out):
     held[0:8] = tails[1].astype(F32)[8:16]
     held[8:16] = tails[2].astype(F32)[8:16]
     held[16:18] = tails[0].astype(F32)[14:16]
-    held[18:20] = tails[4].astype(F32)[14:16]
-    held[20:22] = tails[5].astype(F32)[14:16]
+    held[18:20] = key[ROWS - 16 : ROWS].astype(F32)[14:16]
+    held[20:22] = value[ROWS - 16 : ROWS].astype(F32)[14:16]
     held[22:24] = tails[3].astype(F32)[14:16]
+    held[24:32] = jnp.zeros_like(held[24:32])
     out[...] = held[...].astype(BF16)
 
 
+def rim_kernel(rim, out):
+    out[...] = rim[...]
+
+
 CHUNK = 4
 
 
-def states_kernel(key_hbm, value_hbm, feature_hbm, rate_hbm, kept_hbm, sent_hbm, key, value, feature, rate, kept, sent, wide, fresh, sems, outs):
+def states_kernel(
+    key_hbm, value_hbm, feature_hbm, rate_hbm, seg, sek, sev, lig, kept_hbm, sent_hbm, rim, key, value, feature, rate, kept, sent, packed, wide, fresh, tails, held, sems, outs, tail_sems
+):
     width = key.shape[1]
     chunks = width // (CHUNK * LANES)
 
@@ -115,14 +117,17 @@
         span = piece(width, chunks, index)
         owners = pl.ds(index * (CHUNK // 2), CHUNK // 2)
         return [
-            pltpu.make_async_copy(sent.at[owners], sent_hbm.at[owners], outs.at[2 * index]),
+            pltpu.make_async_copy(packed.at[owners], sent_hbm.at[owners], outs.at[2 * index]),
             pltpu.make_async_copy(kept.at[:, :, span], kept_hbm.at[:, :, span], outs.at[2 * index + 1]),
         ]
 
+    for copy in large(0):
+        copy.start()
     small = [started(feature_hbm, feature, sems.at[0]), started(rate_hbm, rate, sems.at[1])]
-    for index in range(chunks):
+    for index in range(1, chunks):
         for copy in large(index):
             copy.start()
+    last = [started(ref.at[ROWS - 16 : ROWS], tails.at[i], tail_sems.at[i]) for i, ref in enumerate((seg, sek, sev, lig))]
     for copy in small:
         copy.wait()
 
@@ -168,27 +173,27 @@
         for part in range(CHUNK):
             half = slice((part % 2) * LANES, (part % 2 + 1) * LANES)
             sent[index * (CHUNK // 2) + part // 2, 0:MODES, half] = states[part]
+        for owner in range(CHUNK // 2):
+            packed[index * (CHUNK // 2) + owner] = sent[index * (CHUNK // 2) + owner].astype(BF16)
         for copy in leaving(index):
             copy.start()
 
     over(chunks, chunk)
+    for copy in last:
+        copy.wait()
+    fill_rim(tails, key, value, held, rim)
     for index in range(chunks):
         for copy in leaving(index):
             copy.wait()
 
 
 def first_two(taps, own, before):
-    def pair(base, tap):
-        zero, one = own[base : base + 1], own[base + 1 : base + 2]
-        two_ago, one_ago = before[base : base + 1], before[base + 1 : base + 2]
-        return (
-            tap[0] * zero + tap[1] * one_ago + tap[2] * two_ago,
-            tap[0] * one + tap[1] * zero + tap[2] * one_ago,
-        )
-
-    k0, k1 = pair(0, taps[0])
-    v0, v1 = pair(2, taps[1])
-    return ((k0 * v0).astype(BF16).astype(F32), (k1 * v1).astype(BF16).astype(F32))
+    row = lax.broadcasted_iota(jnp.int32, own.shape, 0)
+    two = pltpu.roll(before, 4, 0)
+    one = jnp.where(row % 2 == 0, pltpu.roll(two, 7, 0), pltpu.roll(own, 1, 0))
+    featurized = taps[0] * own + taps[1] * one + taps[2] * two
+    u = (featurized * pltpu.roll(featurized, 6, 0)).astype(BF16).astype(F32)
+    return u[0:1], u[1:2]
 
 
 def owned_lanes(chips, width):
@@ -197,25 +202,30 @@
 
 
 def taps_of(feature):
-    return [[feature[j, s : s + 1] for j in range(3)] for s in (1, 2)]
-
-
-def group_kernel(chips, came, feature, rate, sent_hbm, full_hbm, sent, full, sems):
+    width = feature.shape[2]
+    row = lax.broadcasted_iota(jnp.int32, (8, width), 0)
+    return [jnp.where(row < 2, feature[j, 1:2], feature[j, 2:3]) for j in range(3)]
+
+
+def group_kernel(chips, came, feature, rate, sent_hbm, full_hbm, own, sent, full, sems):
     lanes = owned_lanes(chips, came.shape[2])
-    taps = [[feature[j, s : s + 1, lanes] for j in range(3)] for s in (1, 2)]
+    own[...] = feature[:, :, lanes]
+    taps = taps_of(own)
     pace = rate[:, lanes]
     e_block = jnp.exp(-float(ROWS) * pace)
     e_first = jnp.exp(-float(ROWS - 1) * pace)
     e_second = jnp.exp(-float(ROWS - 2) * pace)
     peers = came.shape[0]
-    total = came[0, 0:MODES]
+    blocks = [came[i].astype(F32) for i in range(peers)]
+    total = blocks[0][0:MODES]
     full[0] = total
     for i in range(1, peers):
-        u0, u1 = first_two(taps, came[i, 16:20], came[i - 1, 20:24])
-        mine = came[i, 0:MODES] + e_first * u0 + e_second * u1
+        u0, u1 = first_two(taps, blocks[i][16:24], blocks[i - 1][16:24])
+        mine = blocks[i][0:MODES] + e_first * u0 + e_second * u1
         full[i] = mine
         total = e_block * total + mine
-    rims = jnp.concatenate([came[0, 16:20], came[peers - 1, 20:24]], axis=0)
+    row = lax.broadcasted_iota(jnp.int32, (8, came.shape[2]), 0)
+    rims = jnp.where(row < 4, blocks[0][16:24], blocks[peers - 1][16:24])
     sent[...] = jnp.concatenate([total, rims], axis=0).astype(BF16)
     copies = [started(sent, sent_hbm.at[i], sems.at[i]) for i in range(sent_hbm.shape[0])]
     copies.append(started(full, full_hbm, sems.at[sent_hbm.shape[0]]))
@@ -223,12 +233,10 @@
         copy.wait()
 
 
-def carry_kernel(chips, came, full_hbm, feature_hbm, rate, out_hbm, full, out, feature, sems):
+def carry_kernel(chips, came, full_hbm, feature, rate, out_hbm, full, out, sems):
     lanes = owned_lanes(chips, came.shape[2])
     arriving = started(full_hbm, full, sems.at[0])
-    tapping = started(feature_hbm.at[:, :, lanes], feature, sems.at[2])
     pace = rate[:, lanes]
-    tapping.wait()
     taps = taps_of(feature)
     me = lax.axis_index(FAR)
     peers = full.shape[0]
@@ -240,22 +248,22 @@
     e_first = jnp.exp(-float(ROWS - 1) * pace)
     e_second = jnp.exp(-float(ROWS - 2) * pace)
     carry = jnp.zeros_like(pace)
-    before = jnp.zeros((4, pace.shape[1]), F32)
+    before = jnp.zeros((8, pace.shape[1]), F32)
     own0 = jnp.zeros((1, pace.shape[1]), F32)
     own1 = own0
     for i in range(came.shape[0]):
         block = came[i].astype(F32)
-        u0, u1 = first_two(taps, block[16:20], before)
-        before = block[20:24]
+        u0, u1 = first_two(taps, block[16:24], before)
+        before = block[16:24]
         total = block[0:MODES] + g_first * u0 + g_second * u1
         carry = jnp.where(i < me, e_group * carry + total, carry)
         own0 = jnp.where(i == me, u0, own0)
         own1 = jnp.where(i == me, u1, own1)
     arriving.wait()
-    out[0] = carry
+    out[0] = carry.astype(BF16)
     carry = e_block * carry + (full[0] + e_first * own0 + e_second * own1)
     for i in range(1, peers):
-        out[i] = carry
+        out[i] = carry.astype(BF16)
         carry = e_block * carry + full[i]
     started(out, out_hbm, sems.at[1]).wait()
 
@@ -478,7 +486,7 @@
 
     def one(owner, slot):
         lanes = lanes_at(owner * 2 + slot)
-        state = came[owner, :, slot * LANES : (slot + 1) * LANES]
+        state = came[owner, :, slot * LANES : (slot + 1) * LANES].astype(F32)
         pace = rate[:, lanes]
         jump = jnp.exp(-float(STEP) * pace)
         for g in range(GROUPS):
@@ -531,11 +539,11 @@
     rim_room = room(32, width, dtype=BF16)
     feature_room = room(*li_feature.shape)
 
-    kept, sent = call(
+    kept, sent, rim = call(
         states_kernel,
         "states",
-        [HBM] * 4,
-        [(slow(GROUPS, MODES, width), HBM), (slow(near, 24, part), HBM)],
+        [HBM] * 8,
+        [(slow(GROUPS, MODES, width), HBM), (slow(near, 24, part, dtype=BF16), HBM), (fast(32, width, dtype=BF16), AUTO)],
         [
             stream,
             stream,
@@ -543,36 +551,32 @@
             room(MODES, width),
             room(GROUPS, MODES, width),
             room(near, 24, part),
+            room(near, 24, part, dtype=BF16),
             room(2, 3, 8 + ROWS, LANES),
             room(CHUNK, ROWS, LANES),
+            room(4, 16, width, dtype=BF16),
+            room(32, width),
             dma((2 + 2 * (width // (CHUNK * LANES)),)),
             dma((2 * (width // (CHUNK * LANES)),)),
+            dma((4,)),
         ],
         12000000,
         3000000,
-    )(li_key, li_value, li_feature, li_rate)
+    )(li_key, li_value, li_feature, li_rate, se_gate, se_key, se_value, li_gate)
 
     came = swap(sent, NEAR)
-    rim = call(
-        rim_kernel,
-        "rim",
-        [HBM] * 7,
-        [(fast(32, width, dtype=BF16), AUTO)],
-        [room(6, 16, width, dtype=BF16), room(32, width), dma((6,))],
-        1000000,
-        500000,
-    )(se_gate, se_key, se_value, li_gate, li_key, li_value, kept)
+    rim = call(rim_kernel, "rim", [AUTO], [(fast(32, width, dtype=BF16), AUTO)], [], 1000000, 500000)(rim)
     weight = li_residue * jnp.sqrt(-jnp.expm1(-2.0 * li_rate))
     reach = call(
         reach_kernel, "reach", [AUTO] * 2, [(fast(MODES, HALF, width), AUTO)], [], 3000000, 2000000
     )(li_rate, weight)
     came, reach = lax.optimization_barrier((came, reach))
 
-    group, full = call(
+    group, full, taps = call(
         functools.partial(group_kernel, chips),
         "group",
         [AUTO] * 3,
-        [(slow(far, 24, part, dtype=BF16), HBM), (slow(near, MODES, part), HBM)],
+        [(slow(far, 24, part, dtype=BF16), HBM), (slow(near, MODES, part), HBM), (fast(3, 3, part), AUTO)],
         [room(24, part, dtype=BF16), room(near, MODES, part), dma((far + 1,))],
         500000,
         500000,
@@ -611,12 +615,12 @@
     states = call(
         functools.partial(carry_kernel, chips),
         "carry",
-        [AUTO, HBM, HBM, AUTO],
-        [(slow(near, MODES, part), HBM)],
-        [room(near, MODES, part), room(near, MODES, part), room(3, 3, part), dma((3,))],
+        [AUTO, HBM, AUTO, AUTO],
+        [(slow(near, MODES, part, dtype=BF16), HBM)],
+        [room(near, MODES, part), room(near, MODES, part, dtype=BF16), dma((2,))],
         500000,
         500000,
-    )(groups, full, li_feature, li_rate)
+    )(groups, full, taps, li_rate)
 
     back = swap(states, NEAR)
     se_out = call(

time: 48.9 us -> 47.7 us (0.975)
  Pallas kernels: 18.9 us -> 17.7 us
    pallas_call x8, Pallas kernels: 18.9 us -> 17.7 us  [outer(): inner(*[pltpu.with_memory_space_constraint(v, pltpu.HBM) if spec is HBM e...]
  transfers between devices with their start and end apart: 4 -> 4, of which waited for: 3 -> 3; matrix products, arithmetic and copies ran while one was open for 0% -> 0% of each run, Pallas kernels for 23% -> 21%
where the time goes in v2:
time: 47.7 us; the launch traced here: 47.3 us
  starting transfers between devices  23.7 us (50%)
  Pallas kernels  17.7 us (37%)
  waiting for transfers between devices  4.37 us (9%)
  between operations  0.76 us (2%)
  local copies, waits for them, and re-layouts  0.65 us (1%)
    all_to_all x3, starting transfers between devices, shards(): lax.all_to_all(value, axis, split_axis=0, concat_axis=0, tiled=True)  20.4 us
    pallas_call x8, Pallas kernels, outer(): inner(*[pltpu.with_memory_space_constraint(v, pltpu.HBM) if spec is HBM e...  17.7 us
    all_to_all x3, waiting for transfers between devices, shards(): lax.all_to_all(value, axis, split_axis=0, concat_axis=0, tiled=True)  4.37 us
    ppermute x1, starting transfers between devices, shards(): halo = lax.ppermute(rim, PART, [(i, i + 1) for i in range(count - 1)])  3.28 us
  transfers between devices with their start and end apart: 4, of which 3 were waited for; matrix products, arithmetic and copies ran while one was open for 0% of the time, Pallas kernels for 21%

profile of v2, /device:TPU:1, one launch (start us, length us, event | category | flops | bytes accessed | tf_op | source)
XLA Modules:
  0.0 47.3 jit_solution(4505195698602274233)
XLA Ops:
  0.6 0.0 copy-start.1
  0.6 0.0 copy-start
  0.7 0.0 copy-start.2
  0.7 4.0 %states.1 = (f32[8,16,2048]{2,1,0:T(8,128)}, bf16[8,24,256]{2,1,0:T(8,128)(2,1)}, bf16[32,2048]{1,0:T(8,128)(2,1)S(1)}) custom-call(bf16[128,2048]{1,0:T(8,128)(2,1)} %key_hbm.5, bf16[128,2048]{1,0:T(8,128)(2,1)} %value_hbm.5, f32[3,3,2048]{2,1,0:T(4,128)} %feature_hbm.5, f32[16,2048]{1,0:T(8,128)} %rate.9, bf16[128,2048]{1,0:T(8,128)(2,1)} %gate_hbm.2, ...), custom_call_target="tpu_custom_call" | custom-call | flops 12000000 | bytes 3000000 | tf_op jit(solution)/shard_map/states/pallas_call | solution.py:59
  4.6 10.2 %all-to-all-start = ((bf16[8,24,256]{2,1,0:T(8,128)(2,1)}), bf16[8,24,256]{2,1,0:T(8,128)(2,1)S(1)}, u32[]{:S(2)}, u32[]{:S(2)}) async-start(bf16[8,24,256]{2,1,0:T(8,128)(2,1)} %get-tuple-element.13), calls=%async_computation | async-start | bytes 196608 | tf_op jit(solution)/shard_map/all_to_all | solution.py:535
  14.8 3.3 %collective-permute-start = (bf16[32,2048]{1,0:T(8,128)(2,1)S(1)}, bf16[32,2048]{1,0:T(8,128)(2,1)S(1)}, u32[]{:S(2)}, u32[]{:S(2)}) collective-permute-start(bf16[32,2048]{1,0:T(8,128)(2,1)S(1)} %rim.1), channel_id=1, source_target_pairs={{0,1},{1,2},{2,3},{3,4},{4,5},{5,6},{6,7},{7,8},{8,9},{9,10},{10,1... | collective-permute-start | bytes 393224 | tf_op jit(solution)/shard_map/ppermute | solution.py:587
  18.1 0.0 copy-done
  18.1 0.0 copy-done.2
  18.1 0.1 sqrt_multiply_fusion.weight
  18.2 0.3 reach.1
  18.6 1.2 %all-to-all-done.came = bf16[8,24,256]{2,1,0:T(8,128)(2,1)S(1)} async-done(((bf16[8,24,256]{2,1,0:T(8,128)(2,1)}), bf16[8,24,256]{2,1,0:T(8,128)(2,1)S(1)}, u32[]{:S(2)}, u32[]{:S(2)}) %all-to-all-start) | async-done | bytes 98336 | tf_op jit(solution)/shard_map/all_to_all | solution.py:535
  19.8 0.0 copy-done.1
  19.8 0.9 %group.1 = (bf16[16,24,256]{2,1,0:T(8,128)(2,1)}, f32[8,16,256]{2,1,0:T(8,128)}, f32[3,3,256]{2,1,0:T(4,128)S(1)}) custom-call(bf16[8,24,256]{2,1,0:T(8,128)(2,1)S(1)} %all-to-all-done.came, f32[3,3,2048]{2,1,0:T(4,128)S(1)} %copy-done.1, f32[16,2048]{1,0:T(8,128)S(1)} %copy-done), custom_call_target="tpu_custom_call" | custom-call | flops 500000 | bytes 500000 | tf_op jit(solution)/shard_map/group/pallas_call | solution.py:59
  20.8 4.0 %all-to-all-start.1 = ((bf16[16,24,256]{2,1,0:T(8,128)(2,1)}), bf16[16,24,256]{2,1,0:T(8,128)(2,1)S(1)}, u32[]{:S(2)}, u32[]{:S(2)}) async-start(bf16[16,24,256]{2,1,0:T(8,128)(2,1)} %get-tuple-element.15), calls=%async_computation.1 | async-start | bytes 393216 | tf_op jit(solution)/shard_map/all_to_all | solution.py:535
  24.8 0.0 collective-permute-done.rim_hbm
  24.8 0.0 copy-start.3
  24.8 0.6 %copy-done.3 = bf16[32,2048]{1,0:T(8,128)(2,1)} copy-done((bf16[32,2048]{1,0:T(8,128)(2,1)}, bf16[32,2048]{1,0:T(8,128)(2,1)S(1)}, u32[]{:S(2)}) %copy-start.3) | copy-done | bytes 131096
  25.5 4.9 %local.1 = f32[256,2048]{1,0:T(8,128)S(1)} custom-call(bf16[128,2048]{1,0:T(8,128)(2,1)} %gate_hbm.3, bf16[128,2048]{1,0:T(8,128)(2,1)} %key_hbm.5, bf16[128,2048]{1,0:T(8,128)(2,1)} %value_hbm.5, bf16[32,2048]{1,0:T(8,128)(2,1)} %copy-done.3, f32[3,3,2048]{2,1,0:T(4,128)} %feature_hbm.5, f32[1,2048]{1,0:T(1,128)} %bitcast.1, ...), custom_call_target="tpu_custom_call" | custom-call | flops 49999998976 | bytes 3000000 | tf_op jit(solution)/shard_map/local/pallas_call | solution.py:59
  30.4 1.9 %all-to-all-done.1.came = bf16[16,24,256]{2,1,0:T(8,128)(2,1)S(1)} async-done(((bf16[16,24,256]{2,1,0:T(8,128)(2,1)}), bf16[16,24,256]{2,1,0:T(8,128)(2,1)S(1)}, u32[]{:S(2)}, u32[]{:S(2)}) %all-to-all-start.1) | async-done | bytes 196640 | tf_op jit(solution)/shard_map/all_to_all | solution.py:535
  32.3 1.6 %carry.1 = bf16[8,16,256]{2,1,0:T(8,128)(2,1)} custom-call(bf16[16,24,256]{2,1,0:T(8,128)(2,1)S(1)} %all-to-all-done.1.came, f32[8,16,256]{2,1,0:T(8,128)} %get-tuple-element.19.full_hbm, f32[3,3,256]{2,1,0:T(4,128)S(1)} %get-tuple-element.20.feature, f32[16,2048]{1,0:T(8,128)S(1)} %copy-done), custom_call_target="tpu_custom_call" | custom-call | flops 500000 | bytes 500000 | tf_op jit(solution)/shard_map/carry/pallas_call | solution.py:59
  33.9 6.2 %all-to-all-start.2 = ((bf16[8,16,256]{2,1,0:T(8,128)(2,1)}), bf16[8,16,256]{2,1,0:T(8,128)(2,1)S(1)}, u32[]{:S(2)}, u32[]{:S(2)}) async-start(bf16[8,16,256]{2,1,0:T(8,128)(2,1)} %carry.1), calls=%async_computation.2 | async-start | bytes 131072 | tf_op jit(solution)/shard_map/all_to_all | solution.py:535
  40.1 3.8 %short.1 = bf16[128,2048]{1,0:T(8,128)(2,1)} custom-call(bf16[128,2048]{1,0:T(8,128)(2,1)} %gate_hbm.2, bf16[128,2048]{1,0:T(8,128)(2,1)} %key_hbm.4, bf16[128,2048]{1,0:T(8,128)(2,1)} %value_hbm.4, bf16[32,2048]{1,0:T(8,128)(2,1)} %copy-done.3, f32[3,3,2048]{2,1,0:T(4,128)} %feature_hbm.4, f32[7,2048]{1,0:T(8,128)} %taps_hbm.1), custom_call_target="tpu_custom_call" | custom-call | flops 12000000 | bytes 2000000 | tf_op jit(solution)/shard_map/short/pallas_call | solution.py:59
  43.9 1.2 %all-to-all-done.2.came = bf16[8,16,256]{2,1,0:T(8,128)(2,1)S(1)} async-done(((bf16[8,16,256]{2,1,0:T(8,128)(2,1)}), bf16[8,16,256]{2,1,0:T(8,128)(2,1)S(1)}, u32[]{:S(2)}, u32[]{:S(2)}) %all-to-all-start.2) | async-done | bytes 65568 | tf_op jit(solution)/shard_map/all_to_all | solution.py:535
  45.1 2.2 %finish.1 = bf16[128,2048]{1,0:T(8,128)(2,1)} custom-call(bf16[8,16,256]{2,1,0:T(8,128)(2,1)S(1)} %all-to-all-done.2.came, f32[256,2048]{1,0:T(8,128)S(1)} %local.1, f32[16,8,2048]{2,1,0:T(8,128)S(1)} %reach.1, f32[16,2048]{1,0:T(8,128)S(1)} %copy-done), custom_call_target="tpu_custom_call" | custom-call | flops 10000000 | bytes 5000000 | tf_op jit(solution)/shard_map/finish/pallas_call | solution.py:59
  (1 shorter events, 0.0 us)
Async XLA Ops:
  0.6 19.2 %copy-start.1 = (f32[3,3,2048]{2,1,0:T(4,128)S(1)}, f32[3,3,2048]{2,1,0:T(4,128)}, u32[]{:S(2)}) copy-start(f32[3,3,2048]{2,1,0:T(4,128)} %feature_hbm.5) | copy-start | bytes 221188
  0.6 17.5 %copy-start = (f32[16,2048]{1,0:T(8,128)S(1)}, f32[16,2048]{1,0:T(8,128)}, u32[]{:S(2)}) copy-start(f32[16,2048]{1,0:T(8,128)} %rate.9) | copy-start | bytes 393220
  0.7 17.5 %copy-start.2 = (f32[16,2048]{1,0:T(8,128)S(1)}, f32[16,2048]{1,0:T(8,128)}, u32[]{:S(2)}) copy-start(f32[16,2048]{1,0:T(8,128)} %param.21) | copy-start | bytes 393220
  4.6 15.2 %all-to-all-start = ((bf16[8,24,256]{2,1,0:T(8,128)(2,1)}), bf16[8,24,256]{2,1,0:T(8,128)(2,1)S(1)}, u32[]{:S(2)}, u32[]{:S(2)}) async-start(bf16[8,24,256]{2,1,0:T(8,128)(2,1)} %get-tuple-element.13), calls=%async_computation | async-start | bytes 196608 | tf_op jit(solution)/shard_map/all_to_all | solution.py:535
  14.8 10.0 %collective-permute-start = (bf16[32,2048]{1,0:T(8,128)(2,1)S(1)}, bf16[32,2048]{1,0:T(8,128)(2,1)S(1)}, u32[]{:S(2)}, u32[]{:S(2)}) collective-permute-start(bf16[32,2048]{1,0:T(8,128)(2,1)S(1)} %rim.1), channel_id=1, source_target_pairs={{0,1},{1,2},{2,3},{3,4},{4,5},{5,6},{6,7},{7,8},{8,9},{9,10},{10,1... | collective-permute-start | bytes 393224 | tf_op jit(solution)/shard_map/ppermute | solution.py:587
  20.8 11.5 %all-to-all-start.1 = ((bf16[16,24,256]{2,1,0:T(8,128)(2,1)}), bf16[16,24,256]{2,1,0:T(8,128)(2,1)S(1)}, u32[]{:S(2)}, u32[]{:S(2)}) async-start(bf16[16,24,256]{2,1,0:T(8,128)(2,1)} %get-tuple-element.15), calls=%async_computation.1 | async-start | bytes 393216 | tf_op jit(solution)/shard_map/all_to_all | solution.py:535
  24.8 0.6 %copy-start.3 = (bf16[32,2048]{1,0:T(8,128)(2,1)}, bf16[32,2048]{1,0:T(8,128)(2,1)S(1)}, u32[]{:S(2)}) copy-start(bf16[32,2048]{1,0:T(8,128)(2,1)S(1)} %collective-permute-done.rim_hbm) | copy-start | bytes 393220
  33.9 11.2 %all-to-all-start.2 = ((bf16[8,16,256]{2,1,0:T(8,128)(2,1)}), bf16[8,16,256]{2,1,0:T(8,128)(2,1)S(1)}, u32[]{:S(2)}, u32[]{:S(2)}) async-start(bf16[8,16,256]{2,1,0:T(8,128)(2,1)} %carry.1), calls=%async_computation.2 | async-start | bytes 131072 | tf_op jit(solution)/shard_map/all_to_all | solution.py:535

commit v3 on v2

--- a/solution.py
+++ b/solution.py
@@ -487,17 +487,17 @@
     def one(owner, slot):
         lanes = lanes_at(owner * 2 + slot)
         state = came[owner, :, slot * LANES : (slot + 1) * LANES].astype(F32)
-        pace = rate[:, lanes]
-        jump = jnp.exp(-float(STEP) * pace)
+        rows[slot, 0:MODES] = state
+        rows[slot, MODES : 2 * MODES] = jnp.exp(-float(HALF) * rate[:, lanes])
+        totals = [local[k * HALF : (k + 1) * HALF, lanes] for k in range(ROWS // HALF)]
+        for m in range(MODES):
+            term = reach[m, :, lanes] * rows[slot, m : m + 1]
+            hop = jnp.broadcast_to(rows[slot, MODES + m : MODES + m + 1], (HALF, LANES))
+            for k in range(ROWS // HALF):
+                totals[k] = totals[k] + term
+                term = term * hop
         for g in range(GROUPS):
-            rows[slot, g * MODES : (g + 1) * MODES] = state
-            state = state * jump
-        rows[slot, GROUPS * MODES : (GROUPS + 1) * MODES] = jnp.exp(-float(HALF) * pace)
-        low = [local[g * STEP : g * STEP + HALF, lanes] for g in range(GROUPS)]
-        high = [local[g * STEP + HALF : (g + 1) * STEP, lanes] for g in range(GROUPS)]
-        add_modes(low, high, reach, rows, slot, lanes)
-        for g in range(GROUPS):
-            total = local[ROWS + g * STEP : ROWS + (g + 1) * STEP, lanes] * jnp.concatenate([low[g], high[g]], axis=0)
+            total = local[ROWS + g * STEP : ROWS + (g + 1) * STEP, lanes] * jnp.concatenate(totals[2 * g : 2 * g + 2], axis=0)
             out[g * STEP : (g + 1) * STEP, lanes] = total.astype(BF16)
 
     def some(index):
@@ -651,7 +651,7 @@
         "finish",
         [AUTO] * 4,
         [(slow(ROWS, width, dtype=BF16), HBM)],
-        [stream, room(2, (GROUPS + 1) * MODES, LANES), dma((FINISH_PIECES,))],
+        [stream, room(2, 2 * MODES, LANES), dma((FINISH_PIECES,))],
         10000000,
         5000000,
     )(back, local, reach, li_rate)

time: 47.7 us -> 47.6 us (level)
  no operation moved by 1% of the time
where the time goes in v3:
time: 47.6 us; the launch traced here: 47.1 us
  starting transfers between devices  23.7 us (50%)
  Pallas kernels  17.6 us (37%)
  waiting for transfers between devices  4.37 us (9%)
  between operations  0.76 us (2%)
  local copies, waits for them, and re-layouts  0.65 us (1%)
    all_to_all x3, starting transfers between devices, shards(): lax.all_to_all(value, axis, split_axis=0, concat_axis=0, tiled=True)  20.4 us
    pallas_call x8, Pallas kernels, outer(): inner(*[pltpu.with_memory_space_constraint(v, pltpu.HBM) if spec is HBM e...  17.6 us
    all_to_all x3, waiting for transfers between devices, shards(): lax.all_to_all(value, axis, split_axis=0, concat_axis=0, tiled=True)  4.37 us
    ppermute x1, starting transfers between devices, shards(): halo = lax.ppermute(rim, PART, [(i, i + 1) for i in range(count - 1)])  3.28 us
  transfers between devices with their start and end apart: 4, of which 3 were waited for; matrix products, arithmetic and copies ran while one was open for 0% of the time, Pallas kernels for 21%

profile of v3, /device:TPU:1, one launch (start us, length us, event | category | flops | bytes accessed | tf_op | source)
XLA Modules:
  0.0 47.1 jit_solution(11177143239493806246)
XLA Ops:
  0.6 0.0 copy-start.1
  0.6 0.0 copy-start
  0.7 0.0 copy-start.2
  0.7 4.0 %states.1 = (f32[8,16,2048]{2,1,0:T(8,128)}, bf16[8,24,256]{2,1,0:T(8,128)(2,1)}, bf16[32,2048]{1,0:T(8,128)(2,1)S(1)}) custom-call(bf16[128,2048]{1,0:T(8,128)(2,1)} %key_hbm.5, bf16[128,2048]{1,0:T(8,128)(2,1)} %value_hbm.5, f32[3,3,2048]{2,1,0:T(4,128)} %feature_hbm.5, f32[16,2048]{1,0:T(8,128)} %rate.9, bf16[128,2048]{1,0:T(8,128)(2,1)} %gate_hbm.2, ...), custom_call_target="tpu_custom_call" | custom-call | flops 12000000 | bytes 3000000 | tf_op jit(solution)/shard_map/states/pallas_call | solution.py:59
  4.6 10.2 %all-to-all-start = ((bf16[8,24,256]{2,1,0:T(8,128)(2,1)}), bf16[8,24,256]{2,1,0:T(8,128)(2,1)S(1)}, u32[]{:S(2)}, u32[]{:S(2)}) async-start(bf16[8,24,256]{2,1,0:T(8,128)(2,1)} %get-tuple-element.13), calls=%async_computation | async-start | bytes 196608 | tf_op jit(solution)/shard_map/all_to_all | solution.py:535
  14.8 3.3 %collective-permute-start = (bf16[32,2048]{1,0:T(8,128)(2,1)S(1)}, bf16[32,2048]{1,0:T(8,128)(2,1)S(1)}, u32[]{:S(2)}, u32[]{:S(2)}) collective-permute-start(bf16[32,2048]{1,0:T(8,128)(2,1)S(1)} %rim.1), channel_id=1, source_target_pairs={{0,1},{1,2},{2,3},{3,4},{4,5},{5,6},{6,7},{7,8},{8,9},{9,10},{10,1... | collective-permute-start | bytes 393224 | tf_op jit(solution)/shard_map/ppermute | solution.py:587
  18.1 0.0 copy-done
  18.1 0.0 copy-done.2
  18.1 0.1 sqrt_multiply_fusion.weight
  18.2 0.3 reach.1
  18.6 1.2 %all-to-all-done.came = bf16[8,24,256]{2,1,0:T(8,128)(2,1)S(1)} async-done(((bf16[8,24,256]{2,1,0:T(8,128)(2,1)}), bf16[8,24,256]{2,1,0:T(8,128)(2,1)S(1)}, u32[]{:S(2)}, u32[]{:S(2)}) %all-to-all-start) | async-done | bytes 98336 | tf_op jit(solution)/shard_map/all_to_all | solution.py:535
  19.8 0.0 copy-done.1
  19.8 0.9 %group.1 = (bf16[16,24,256]{2,1,0:T(8,128)(2,1)}, f32[8,16,256]{2,1,0:T(8,128)}, f32[3,3,256]{2,1,0:T(4,128)S(1)}) custom-call(bf16[8,24,256]{2,1,0:T(8,128)(2,1)S(1)} %all-to-all-done.came, f32[3,3,2048]{2,1,0:T(4,128)S(1)} %copy-done.1, f32[16,2048]{1,0:T(8,128)S(1)} %copy-done), custom_call_target="tpu_custom_call" | custom-call | flops 500000 | bytes 500000 | tf_op jit(solution)/shard_map/group/pallas_call | solution.py:59
  20.8 4.0 %all-to-all-start.1 = ((bf16[16,24,256]{2,1,0:T(8,128)(2,1)}), bf16[16,24,256]{2,1,0:T(8,128)(2,1)S(1)}, u32[]{:S(2)}, u32[]{:S(2)}) async-start(bf16[16,24,256]{2,1,0:T(8,128)(2,1)} %get-tuple-element.15), calls=%async_computation.1 | async-start | bytes 393216 | tf_op jit(solution)/shard_map/all_to_all | solution.py:535
  24.8 0.0 collective-permute-done.rim_hbm
  24.8 0.0 copy-start.3
  24.8 0.6 %copy-done.3 = bf16[32,2048]{1,0:T(8,128)(2,1)} copy-done((bf16[32,2048]{1,0:T(8,128)(2,1)}, bf16[32,2048]{1,0:T(8,128)(2,1)S(1)}, u32[]{:S(2)}) %copy-start.3) | copy-done | bytes 131096
  25.5 4.9 %local.1 = f32[256,2048]{1,0:T(8,128)S(1)} custom-call(bf16[128,2048]{1,0:T(8,128)(2,1)} %gate_hbm.3, bf16[128,2048]{1,0:T(8,128)(2,1)} %key_hbm.5, bf16[128,2048]{1,0:T(8,128)(2,1)} %value_hbm.5, bf16[32,2048]{1,0:T(8,128)(2,1)} %copy-done.3, f32[3,3,2048]{2,1,0:T(4,128)} %feature_hbm.5, f32[1,2048]{1,0:T(1,128)} %bitcast.1, ...), custom_call_target="tpu_custom_call" | custom-call | flops 49999998976 | bytes 3000000 | tf_op jit(solution)/shard_map/local/pallas_call | solution.py:59
  30.4 1.9 %all-to-all-done.1.came = bf16[16,24,256]{2,1,0:T(8,128)(2,1)S(1)} async-done(((bf16[16,24,256]{2,1,0:T(8,128)(2,1)}), bf16[16,24,256]{2,1,0:T(8,128)(2,1)S(1)}, u32[]{:S(2)}, u32[]{:S(2)}) %all-to-all-start.1) | async-done | bytes 196640 | tf_op jit(solution)/shard_map/all_to_all | solution.py:535
  32.3 1.6 %carry.1 = bf16[8,16,256]{2,1,0:T(8,128)(2,1)} custom-call(bf16[16,24,256]{2,1,0:T(8,128)(2,1)S(1)} %all-to-all-done.1.came, f32[8,16,256]{2,1,0:T(8,128)} %get-tuple-element.19.full_hbm, f32[3,3,256]{2,1,0:T(4,128)S(1)} %get-tuple-element.20.feature, f32[16,2048]{1,0:T(8,128)S(1)} %copy-done), custom_call_target="tpu_custom_call" | custom-call | flops 500000 | bytes 500000 | tf_op jit(solution)/shard_map/carry/pallas_call | solution.py:59
  33.9 6.2 %all-to-all-start.2 = ((bf16[8,16,256]{2,1,0:T(8,128)(2,1)}), bf16[8,16,256]{2,1,0:T(8,128)(2,1)S(1)}, u32[]{:S(2)}, u32[]{:S(2)}) async-start(bf16[8,16,256]{2,1,0:T(8,128)(2,1)} %carry.1), calls=%async_computation.2 | async-start | bytes 131072 | tf_op jit(solution)/shard_map/all_to_all | solution.py:535
  40.1 3.8 %short.1 = bf16[128,2048]{1,0:T(8,128)(2,1)} custom-call(bf16[128,2048]{1,0:T(8,128)(2,1)} %gate_hbm.2, bf16[128,2048]{1,0:T(8,128)(2,1)} %key_hbm.4, bf16[128,2048]{1,0:T(8,128)(2,1)} %value_hbm.4, bf16[32,2048]{1,0:T(8,128)(2,1)} %copy-done.3, f32[3,3,2048]{2,1,0:T(4,128)} %feature_hbm.4, f32[7,2048]{1,0:T(8,128)} %taps_hbm.1), custom_call_target="tpu_custom_call" | custom-call | flops 12000000 | bytes 2000000 | tf_op jit(solution)/shard_map/short/pallas_call | solution.py:59
  43.9 1.2 %all-to-all-done.2.came = bf16[8,16,256]{2,1,0:T(8,128)(2,1)S(1)} async-done(((bf16[8,16,256]{2,1,0:T(8,128)(2,1)}), bf16[8,16,256]{2,1,0:T(8,128)(2,1)S(1)}, u32[]{:S(2)}, u32[]{:S(2)}) %all-to-all-start.2) | async-done | bytes 65568 | tf_op jit(solution)/shard_map/all_to_all | solution.py:535
  45.1 2.1 %finish.1 = bf16[128,2048]{1,0:T(8,128)(2,1)} custom-call(bf16[8,16,256]{2,1,0:T(8,128)(2,1)S(1)} %all-to-all-done.2.came, f32[256,2048]{1,0:T(8,128)S(1)} %local.1, f32[16,8,2048]{2,1,0:T(8,128)S(1)} %reach.1, f32[16,2048]{1,0:T(8,128)S(1)} %copy-done), custom_call_target="tpu_custom_call" | custom-call | flops 10000000 | bytes 5000000 | tf_op jit(solution)/shard_map/finish/pallas_call | solution.py:59
  (1 shorter events, 0.0 us)
Async XLA Ops:
  0.6 19.2 %copy-start.1 = (f32[3,3,2048]{2,1,0:T(4,128)S(1)}, f32[3,3,2048]{2,1,0:T(4,128)}, u32[]{:S(2)}) copy-start(f32[3,3,2048]{2,1,0:T(4,128)} %feature_hbm.5) | copy-start | bytes 221188
  0.6 17.5 %copy-start = (f32[16,2048]{1,0:T(8,128)S(1)}, f32[16,2048]{1,0:T(8,128)}, u32[]{:S(2)}) copy-start(f32[16,2048]{1,0:T(8,128)} %rate.9) | copy-start | bytes 393220
  0.7 17.5 %copy-start.2 = (f32[16,2048]{1,0:T(8,128)S(1)}, f32[16,2048]{1,0:T(8,128)}, u32[]{:S(2)}) copy-start(f32[16,2048]{1,0:T(8,128)} %param.21) | copy-start | bytes 393220
  4.6 15.2 %all-to-all-start = ((bf16[8,24,256]{2,1,0:T(8,128)(2,1)}), bf16[8,24,256]{2,1,0:T(8,128)(2,1)S(1)}, u32[]{:S(2)}, u32[]{:S(2)}) async-start(bf16[8,24,256]{2,1,0:T(8,128)(2,1)} %get-tuple-element.13), calls=%async_computation | async-start | bytes 196608 | tf_op jit(solution)/shard_map/all_to_all | solution.py:535
  14.8 10.0 %collective-permute-start = (bf16[32,2048]{1,0:T(8,128)(2,1)S(1)}, bf16[32,2048]{1,0:T(8,128)(2,1)S(1)}, u32[]{:S(2)}, u32[]{:S(2)}) collective-permute-start(bf16[32,2048]{1,0:T(8,128)(2,1)S(1)} %rim.1), channel_id=1, source_target_pairs={{0,1},{1,2},{2,3},{3,4},{4,5},{5,6},{6,7},{7,8},{8,9},{9,10},{10,1... | collective-permute-start | bytes 393224 | tf_op jit(solution)/shard_map/ppermute | solution.py:587
  20.8 11.5 %all-to-all-start.1 = ((bf16[16,24,256]{2,1,0:T(8,128)(2,1)}), bf16[16,24,256]{2,1,0:T(8,128)(2,1)S(1)}, u32[]{:S(2)}, u32[]{:S(2)}) async-start(bf16[16,24,256]{2,1,0:T(8,128)(2,1)} %get-tuple-element.15), calls=%async_computation.1 | async-start | bytes 393216 | tf_op jit(solution)/shard_map/all_to_all | solution.py:535
  24.8 0.6 %copy-start.3 = (bf16[32,2048]{1,0:T(8,128)(2,1)}, bf16[32,2048]{1,0:T(8,128)(2,1)S(1)}, u32[]{:S(2)}) copy-start(bf16[32,2048]{1,0:T(8,128)(2,1)S(1)} %collective-permute-done.rim_hbm) | copy-start | bytes 393220
  33.9 11.2 %all-to-all-start.2 = ((bf16[8,16,256]{2,1,0:T(8,128)(2,1)}), bf16[8,16,256]{2,1,0:T(8,128)(2,1)S(1)}, u32[]{:S(2)}, u32[]{:S(2)}) async-start(bf16[8,16,256]{2,1,0:T(8,128)(2,1)} %carry.1), calls=%async_computation.2 | async-start | bytes 131072 | tf_op jit(solution)/shard_map/all_to_all | solution.py:535
